TPU v7x, 512 devices: a whole 4x8x8 slice. The times are simulated.
512 devices in a mesh: depth: 64 (over z_hi, y, core), height: 8 (over z_lo, x).
Axes of the slice: x: 4, y: 8, z: 8 (z_hi: 4, z_lo: 2; z = z_hi * 2 + z_lo), core: 2. Of those that a mesh axis runs over, the one named last changes fastest.
Arguments:
- features: bfloat16 [32, 256, 32, 128], P(None, 'depth', 'height'), may hold values from -6 to 6
- kernel_in: bfloat16 [27648], replicated, may hold values from -0.21875 to 0.21875
- kernel_down: bfloat16 [55296], replicated, may hold values from -0.21875 to 0.21875
- kernel_coarse: bfloat16 [110592], replicated, may hold values from -0.15625 to 0.15625
- kernel_up: bfloat16 [110592], replicated, may hold values from -0.15625 to 0.15625
- kernel_out: bfloat16 [27648], replicated, may hold values from -0.21875 to 0.21875
- projection: bfloat16 [64, 32], replicated, may hold values from -0.75 to 0.75
- biases: float32 [256], replicated, may hold values from -3 to 3
- cotangent: bfloat16 [32, 256, 32, 128], P(None, 'depth', 'height'), may hold values from -6 to 6
Outputs:
- decoded: bfloat16 [32, 256, 32, 128], P(None, 'depth', 'height')
- grad_features: bfloat16 [32, 256, 32, 128], P(None, 'depth', 'height')
- grad_in: float32 [27648], replicated
- grad_down: float32 [55296], replicated
- grad_coarse: float32 [110592], replicated
- grad_up: float32 [110592], replicated
- grad_out: float32 [27648], replicated
- grad_projection: float32 [64, 32], replicated
- grad_biases: float32 [256], replicated
All inputs are finite; a program needn't handle non-finite values.
Results may differ from a plain program's by a relative error of at most 0.025.
Values may be sent and summed in bfloat16 or wider, within the bound.
No kernel may reach another device: no remote copies, remote signals or barrier semaphores. Data moves between devices by JAX's collectives and lax.ppermute only.
A program may use at most 64 MiB of HBM per device.

v0:
```python
import math

import jax
import jax.numpy as jnp
from jax import lax
from jax.sharding import PartitionSpec as P

CH_FINE = 32
CH_MID = 64


def padded_2(cells, sides, width):
    for axis, dim in sides:
        count = lax.axis_size(axis)
        ends = count - 1
        head = lax.slice_in_dim(cells, 0, width, axis=dim)
        tail = lax.slice_in_dim(cells, cells.shape[dim] - width, cells.shape[dim], axis=dim)
        cells = jnp.concatenate(
            [
                lax.ppermute(tail, axis, [(i, (i + 1) % count) for i in range(ends)]),
                cells,
                lax.ppermute(head, axis, [((i + 1) % count, i) for i in range(ends)]),
            ],
            axis=dim,
        )
    return cells


def extend(volume):
    both_ext = padded_2(volume, (("depth", 1), ("height", 2)), 1)
    return jnp.pad(both_ext, ((0, 0), (0, 0), (0, 0), (1, 1)))


def shaped(flat, outs, ins):
    return flat.reshape(3, 3, outs, 3 * ins)


def widened(padded):
    span_w = padded.shape[3] - 2
    pieces = [padded[:, :, :, tap_width : tap_width + span_w] for tap_width in range(3)]
    return jnp.concatenate(pieces, axis=0)


def conv_taps(padded, kern):
    span_d = padded.shape[1] - 2
    span_h = padded.shape[2] - 2
    wide = widened(padded)
    result = None
    for tap_depth in range(3):
        for tap_height in range(3):
            window = wide[:, tap_depth : tap_depth + span_d, tap_height : tap_height + span_h, :]
            term = jnp.einsum(
                "ok,kdhw->odhw",
                kern[tap_depth, tap_height],
                window,
                preferred_element_type=jnp.float32,
            )
            result = term if result is None else result + term
    return result


def kernel_taps(padded, grad):
    span_d = padded.shape[1] - 2
    span_h = padded.shape[2] - 2
    wide = widened(padded)
    rows = []
    for tap_depth in range(3):
        inner = []
        for tap_height in range(3):
            window = wide[:, tap_depth : tap_depth + span_d, tap_height : tap_height + span_h, :]
            inner.append(
                jnp.einsum("odhw,kdhw->ok", grad, window, preferred_element_type=jnp.float32)
            )
        rows.append(jnp.stack(inner))
    return jnp.stack(rows).reshape(-1)


def flipped(kern):
    outs = kern.shape[2]
    ins = kern.shape[3] // 3
    turned = kern.reshape(3, 3, outs, 3, ins)[::-1, ::-1, :, ::-1, :]
    return turned.transpose(0, 1, 4, 3, 2).reshape(3, 3, ins, 3 * outs)


def pool_sum(volume):
    chans, span_d, span_h, span_w = volume.shape
    blocks = volume.astype(jnp.float32).reshape(
        chans, span_d // 2, 2, span_h // 2, 2, span_w // 2, 2
    )
    return jnp.sum(blocks, axis=(2, 4, 6))


def upsample(volume):
    chans, span_d, span_h, span_w = volume.shape
    spread = jnp.broadcast_to(
        volume[:, :, None, :, None, :, None], (chans, span_d, 2, span_h, 2, span_w, 2)
    )
    return spread.reshape(chans, 2 * span_d, 2 * span_h, 2 * span_w)


def silu_grad(value):
    sigma = jax.nn.sigmoid(value)
    return sigma * (1.0 + value * (1.0 - sigma))


def column(vector):
    return vector[:, None, None, None]


def local(
    features,
    kernel_in,
    kernel_down,
    kernel_coarse,
    kernel_up,
    kernel_out,
    projection,
    biases,
    cotangent,
):
    fine = CH_FINE
    middle = CH_MID
    kernel_in = shaped(kernel_in, fine, fine)
    kernel_down = shaped(kernel_down, middle, fine)
    kernel_coarse = shaped(kernel_coarse, middle, middle)
    kernel_up = shaped(kernel_up, middle, middle)
    kernel_out = shaped(kernel_out, fine, fine)
    bias_in = biases[:fine]
    bias_down = biases[fine : fine + middle]
    bias_coarse = biases[fine + middle : fine + 2 * middle]
    bias_up = biases[fine + 2 * middle : fine + 3 * middle]
    bias_out = biases[fine + 3 * middle :]
    bf = jnp.bfloat16
    f32 = jnp.float32
    total_cells = (
        features.shape[1]
        * features.shape[2]
        * features.shape[3]
        * lax.axis_size("depth")
        * lax.axis_size("height")
    )
    scale = 1.0 / math.sqrt(total_cells)
    padded_input = extend(features)
    pre_first = conv_taps(padded_input, kernel_in) + column(bias_in)
    act_first = jax.nn.silu(pre_first).astype(bf)
    pooled_one = (pool_sum(act_first) * 0.125).astype(bf)
    padded_one = extend(pooled_one)
    pre_second = conv_taps(padded_one, kernel_down) + column(bias_down)
    act_second = jax.nn.silu(pre_second).astype(bf)
    pooled_two = (pool_sum(act_second) * 0.125).astype(bf)
    padded_two = extend(pooled_two)
    pre_third = conv_taps(padded_two, kernel_coarse) + column(bias_coarse)
    act_third = jax.nn.silu(pre_third).astype(bf)
    merged = (act_second.astype(f32) + upsample(act_third).astype(f32)).astype(bf)
    padded_merged = extend(merged)
    pre_fourth = conv_taps(padded_merged, kernel_up) + column(bias_up)
    act_fourth = jax.nn.silu(pre_fourth).astype(bf)
    lifted = jnp.einsum("io,idhw->odhw", projection, act_fourth, preferred_element_type=f32)
    skip_sum = (act_first.astype(f32) + upsample(lifted)).astype(bf)
    padded_skip = extend(skip_sum)
    decoded = (conv_taps(padded_skip, kernel_out) + column(bias_out)).astype(bf)
    grad_skip = conv_taps(extend(cotangent), flipped(kernel_out)).astype(bf)
    grad_lift = pool_sum(grad_skip)
    fourth_f32 = act_fourth.astype(f32)
    grad_act4 = jnp.einsum(
        "io,odhw->idhw", projection.astype(f32), grad_lift, precision=lax.Precision.HIGHEST
    )
    grad_pre4 = (grad_act4 * silu_grad(pre_fourth)).astype(bf)
    grad_merged = conv_taps(extend(grad_pre4), flipped(kernel_up))
    grad_pre3 = (pool_sum(grad_merged) * silu_grad(pre_third)).astype(bf)
    grad_pool2 = conv_taps(extend(grad_pre3), flipped(kernel_coarse))
    grad_pre2 = ((grad_merged + upsample(grad_pool2) * 0.125) * silu_grad(pre_second)).astype(bf)
    grad_pool1 = conv_taps(extend(grad_pre2), flipped(kernel_down))
    grad_pre1 = (
        (grad_skip.astype(f32) + upsample(grad_pool1) * 0.125) * silu_grad(pre_first)
    ).astype(bf)
    grad_features = conv_taps(extend(grad_pre1), flipped(kernel_in)).astype(bf)
    local_in = kernel_taps(padded_input, grad_pre1)
    local_down = kernel_taps(padded_one, grad_pre2)
    local_coarse = kernel_taps(padded_two, grad_pre3)
    local_up = kernel_taps(padded_merged, grad_pre4)
    local_out = kernel_taps(padded_skip, cotangent)
    local_projection = jnp.einsum(
        "idhw,odhw->io", fourth_f32, grad_lift, precision=lax.Precision.HIGHEST
    )
    parts = [
        jnp.sum(item.astype(f32), axis=(1, 2, 3))
        for item in (grad_pre1, grad_pre2, grad_pre3, grad_pre4, cotangent)
    ]
    local_biases = jnp.concatenate(parts)
    summed = lax.psum(
        (local_in, local_down, local_coarse, local_up, local_out, local_projection, local_biases),
        ("depth", "height"),
    )
    grad_in, grad_down, grad_coarse, grad_up, grad_out, grad_projection, grad_biases = [
        item * scale for item in summed
    ]
    return (
        decoded,
        grad_features,
        grad_in,
        grad_down,
        grad_coarse,
        grad_up,
        grad_out,
        grad_projection,
        grad_biases,
    )


def solution(mesh):
    placed = (
        P(None, "depth", "height", None),
        P(),
        P(),
        P(),
        P(),
        P(),
        P(),
        P(),
        P(None, "depth", "height", None),
    )
    return jax.shard_map(
        local,
        mesh=mesh,
        in_specs=placed,
        out_specs=(
            P(None, "depth", "height", None),
            P(None, "depth", "height", None),
            P(),
            P(),
            P(),
            P(),
            P(),
            P(),
            P(),
        ),
        check_vma=False,
    )
```

profile of v0, /device:TPU:1, one launch (start us, length us, event | category | flops | bytes accessed | tf_op | source)
XLA Modules:
  0.0 664.2 jit_solution(12565591313136767056)
XLA Ops:
  8.2 4.6 collective-permute-start
  12.8 5.5 collective-permute-start.1
  50.7 4.0 collective-permute-start.22
  60.3 3.4 collective-permute-start.4
  69.0 4.3 collective-permute-start.6
  74.8 3.5 collective-permute-done.7
  81.5 4.5 collective-permute-start.8
  91.0 5.0 collective-permute-start.10
  97.5 5.5 collective-permute-done.11
  105.0 3.1 collective-permute-start.12
  114.1 6.1 collective-permute-start.14
  131.8 3.3 collective-permute-start.24
  137.2 3.2 collective-permute-done.25
  141.1 3.8 collective-permute-start.26
  154.3 5.2 collective-permute-start.28
  164.5 3.4 collective-permute-start.30
  175.7 4.3 collective-permute-start.32
  182.0 3.2 collective-permute-done.33
  185.3 5.0 collective-permute-start.34
  201.8 133.0 %all-reduce.10 = (f32[64,32]{0,1:T(8,128)S(1)}, f32[256]{0:T(256)S(1)}) all-reduce(f32[64,32]{0,1:T(8,128)S(1)} %convolution_bitcast_fusion.38, f32[256]{0:T(256)S(1)} %concatenate.128), channel_id=1, replica_groups=mesh['depth'=64,'height'=8] {'depth','height'}, use_global_device_ids=true, to_apply=%region_11.12 | all-reduce | flops 2304 | bytes 18432 | tf_op jit(solution)/shard_map/psum | solution.py:191
  336.0 3.7 collective-permute-start.16
  342.4 3.6 collective-permute-start.36
  351.3 3.6 collective-permute-start.38
  366.8 285.9 %all-reduce.14.cloned.1.call-done = (f32[27648]{0:T(1024)}, f32[55296]{0:T(1024)}, f32[110592]{0:T(1024)}, f32[110592]{0:T(1024)}, f32[27648]{0:T(1024)}) async-done(((f32[27648]{0:T(1024)}, f32[55296]{0:T(1024)}, f32[110592]{0:T(1024)}, f32[110592]{0:T(1024)}, f32[27648]{0:T(1024)}), (f32[27648]{0:T(1024)}, f32[55296]{0:T(1024)}, f32[110592]{0:T(1024)}, f32[110592]{0:T(1024)}, ...) | async-done | bytes 1327120 | tf_op jit(solution)/shard_map/psum | solution.py:191
  (416 shorter events, 137.8 us)
Async XLA Ops:
  7.2 645.5 %all-reduce.14.cloned.1.call-start = ((), (), s32[]{:S(2)}) async-start(), calls=%async_computation | async-start | bytes 2654208 | tf_op jit(solution)/shard_map/psum | solution.py:191
  8.2 37.6 %collective-permute-start = (bf16[32,1,4,128]{3,0,2,1:T(8,128)(2,1)S(1)}, bf16[32,1,4,128]{3,0,2,1:T(8,128)(2,1)S(1)}, u32[]{:S(2)}, u32[]{:S(2)}) collective-permute-start(bf16[32,1,4,128]{3,0,2,1:T(8,128)(2,1)S(1)} %copy.332), channel_id=1, source_target_pairs={{0,8},{8,16},{16,24},{24,32},{32,40},{40,48},{48,56},{56,64},{64,7... | collective-permute-start | bytes 98312 | tf_op jit(solution)/shard_map/ppermute | solution.py:20
  12.8 33.0 %collective-permute-start.1 = (bf16[32,1,4,128]{3,0,2,1:T(8,128)(2,1)S(1)}, bf16[32,1,4,128]{3,0,2,1:T(8,128)(2,1)S(1)}, u32[]{:S(2)}, u32[]{:S(2)}) collective-permute-start(bf16[32,1,4,128]{3,0,2,1:T(8,128)(2,1)S(1)} %copy.333), channel_id=1, source_target_pairs={{8,0},{16,8},{24,16},{32,24},{40,32},{48,40},{56,48},{64,56},{72,6... | collective-permute-start | bytes 98312 | tf_op jit(solution)/shard_map/ppermute | solution.py:22
  19.1 29.4 %collective-permute-start.20 = (bf16[32,1,4,128]{3,0,2,1:T(8,128)(2,1)S(1)}, bf16[32,1,4,128]{3,0,2,1:T(8,128)(2,1)}, u32[]{:S(2)}, u32[]{:S(2)}) collective-permute-start(bf16[32,1,4,128]{3,0,2,1:T(8,128)(2,1)S(1)} %copy.334), channel_id=1, source_target_pairs={{0,8},{8,16},{16,24},{24,32},{32,40},{40,48},{48,56},{56,64},{64,7... | collective-permute-start | bytes 98312 | tf_op jit(solution)/shard_map/ppermute | solution.py:20
  21.0 28.2 %collective-permute-start.21 = (bf16[32,1,4,128]{3,0,2,1:T(8,128)(2,1)S(1)}, bf16[32,1,4,128]{3,0,2,1:T(8,128)(2,1)}, u32[]{:S(2)}, u32[]{:S(2)}) collective-permute-start(bf16[32,1,4,128]{3,0,2,1:T(8,128)(2,1)S(1)} %copy.335), channel_id=1, source_target_pairs={{8,0},{16,8},{24,16},{32,24},{40,32},{48,40},{56,48},{64,56},{72,6... | collective-permute-start | bytes 98312 | tf_op jit(solution)/shard_map/ppermute | solution.py:22
  45.9 10.1 %collective-permute-start.2 = (bf16[32,6,1,128]{3,0,2,1:T(8,128)(2,1)S(1)}, bf16[32,6,1,128]{3,0,2,1:T(8,128)(2,1)S(1)}, u32[]{:S(2)}, u32[]{:S(2)}) collective-permute-start(bf16[32,6,1,128]{3,0,2,1:T(8,128)(2,1)S(1)} %get-tuple-element.74), channel_id=1, source_target_pairs={{0,1},{1,2},{2,3},{3,4},{4,5},{5,6},{6,7},{8,9},{9,10},{10,11},{11... | collective-permute-start | bytes 147464 | tf_op jit(solution)/shard_map/ppermute | solution.py:20
  47.2 8.8 %collective-permute-start.3 = (bf16[32,6,1,128]{3,0,2,1:T(8,128)(2,1)S(1)}, bf16[32,6,1,128]{3,0,2,1:T(8,128)(2,1)S(1)}, u32[]{:S(2)}, u32[]{:S(2)}) collective-permute-start(bf16[32,6,1,128]{3,0,2,1:T(8,128)(2,1)S(1)} %get-tuple-element.75), channel_id=1, source_target_pairs={{1,0},{2,1},{3,2},{4,3},{5,4},{6,5},{7,6},{9,8},{10,9},{11,10},{12... | collective-permute-start | bytes 147464 | tf_op jit(solution)/shard_map/ppermute | solution.py:22
  50.7 14.9 %collective-permute-start.22 = (bf16[32,6,1,128]{3,0,2,1:T(8,128)(2,1)}, bf16[32,6,1,128]{3,0,2,1:T(8,128)(2,1)S(1)}, u32[]{:S(2)}, u32[]{:S(2)}) collective-permute-start(bf16[32,6,1,128]{3,0,2,1:T(8,128)(2,1)} %get-tuple-element.70), channel_id=1, source_target_pairs={{0,1},{1,2},{2,3},{3,4},{4,5},{5,6},{6,7},{8,9},{9,10},{10,11},{11... | collective-permute-start | bytes 147464 | tf_op jit(solution)/shard_map/ppermute | solution.py:20
  54.7 11.0 %collective-permute-start.23 = (bf16[32,6,1,128]{3,0,2,1:T(8,128)(2,1)}, bf16[32,6,1,128]{3,0,2,1:T(8,128)(2,1)S(1)}, u32[]{:S(2)}, u32[]{:S(2)}) collective-permute-start(bf16[32,6,1,128]{3,0,2,1:T(8,128)(2,1)} %get-tuple-element.71), channel_id=1, source_target_pairs={{1,0},{2,1},{3,2},{4,3},{5,4},{6,5},{7,6},{9,8},{10,9},{11,10},{12... | collective-permute-start | bytes 147464 | tf_op jit(solution)/shard_map/ppermute | solution.py:22
  60.3 7.7 %collective-permute-start.4 = (bf16[32,1,2,64]{0,3,2,1:T(8,128)(2,1)S(1)}, bf16[32,1,2,64]{0,3,2,1:T(8,128)(2,1)S(1)}, u32[]{:S(2)}, u32[]{:S(2)}) collective-permute-start(bf16[32,1,2,64]{0,3,2,1:T(8,128)(2,1)S(1)} %get-tuple-element.102), channel_id=1, source_target_pairs={{0,8},{8,16},{16,24},{24,32},{32,40},{40,48},{48,56},{56,64},{64,7... | collective-permute-start | bytes 24584 | tf_op jit(solution)/shard_map/ppermute | solution.py:20
  81.5 6.6 collective-permute-start.8
  91.0 6.5 collective-permute-start.10
  95.9 7.0 %collective-permute-start.11 = (bf16[64,3,1,32]{0,3,2,1:T(8,128)(2,1)S(1)}, bf16[64,3,1,32]{0,3,2,1:T(8,128)(2,1)S(1)}, u32[]{:S(2)}, u32[]{:S(2)}) collective-permute-start(bf16[64,3,1,32]{0,3,2,1:T(8,128)(2,1)S(1)} %pad_maximum_fusion.25), channel_id=1, source_target_pairs={{1,0},{2,1},{3,2},{4,3},{5,4},{6,5},{7,6},{9,8},{10,9},{11,10},{12... | collective-permute-start | bytes 36872 | tf_op jit(solution)/shard_map/ppermute | solution.py:22
  114.1 10.4 %collective-permute-start.14 = (bf16[64,4,1,64]{0,3,2,1:T(8,128)(2,1)}, bf16[64,4,1,64]{0,3,2,1:T(8,128)(2,1)}, u32[]{:S(2)}, u32[]{:S(2)}) collective-permute-start(bf16[64,4,1,64]{0,3,2,1:T(8,128)(2,1)} %get-tuple-element.86), channel_id=1, source_target_pairs={{0,1},{1,2},{2,3},{3,4},{4,5},{5,6},{6,7},{8,9},{9,10},{10,11},{11... | collective-permute-start | bytes 98312 | tf_op jit(solution)/shard_map/ppermute | solution.py:20
  141.1 7.7 %collective-permute-start.26 = (bf16[64,4,1,64]{0,3,2,1:T(8,128)(2,1)}, bf16[64,4,1,64]{0,3,2,1:T(8,128)(2,1)}, u32[]{:S(2)}, u32[]{:S(2)}) collective-permute-start(bf16[64,4,1,64]{0,3,2,1:T(8,128)(2,1)} %get-tuple-element.80), channel_id=1, source_target_pairs={{0,1},{1,2},{2,3},{3,4},{4,5},{5,6},{6,7},{8,9},{9,10},{10,11},{11... | collective-permute-start | bytes 98312 | tf_op jit(solution)/shard_map/ppermute | solution.py:20
  154.3 8.8 %collective-permute-start.28 = (bf16[64,1,1,32]{0,3,2,1:T(8,128)(2,1)S(1)}, bf16[64,1,1,32]{0,3,2,1:T(8,128)(2,1)S(1)}, u32[]{:S(2)}, u32[]{:S(2)}) collective-permute-start(bf16[64,1,1,32]{0,3,2,1:T(8,128)(2,1)S(1)} %bitcast.1099), channel_id=1, source_target_pairs={{0,8},{8,16},{16,24},{24,32},{32,40},{40,48},{48,56},{56,64},{64,7... | collective-permute-start | bytes 12296 | tf_op jit(solution)/shard_map/ppermute | solution.py:20
  175.7 6.3 collective-permute-start.32
  185.3 7.3 %collective-permute-start.34 = (bf16[64,4,1,64]{0,3,2,1:T(8,128)(2,1)S(1)}, bf16[64,4,1,64]{0,3,2,1:T(8,128)(2,1)S(1)}, u32[]{:S(2)}, u32[]{:S(2)}) collective-permute-start(bf16[64,4,1,64]{0,3,2,1:T(8,128)(2,1)S(1)} %get-tuple-element.78), channel_id=1, source_target_pairs={{0,1},{1,2},{2,3},{3,4},{4,5},{5,6},{6,7},{8,9},{9,10},{10,11},{11... | collective-permute-start | bytes 98312 | tf_op jit(solution)/shard_map/ppermute | solution.py:20
  336.0 12.0 %collective-permute-start.16 = (bf16[32,1,4,128]{3,0,2,1:T(8,128)(2,1)S(1)}, bf16[32,1,4,128]{3,0,2,1:T(8,128)(2,1)S(1)}, u32[]{:S(2)}, u32[]{:S(2)}) collective-permute-start(bf16[32,1,4,128]{3,0,2,1:T(8,128)(2,1)S(1)} %get-tuple-element.84), channel_id=1, source_target_pairs={{0,8},{8,16},{16,24},{24,32},{32,40},{40,48},{48,56},{56,64},{64,7... | collective-permute-start | bytes 98312 | tf_op jit(solution)/shard_map/ppermute | solution.py:20
  339.7 8.3 %collective-permute-start.17 = (bf16[32,1,4,128]{3,0,2,1:T(8,128)(2,1)S(1)}, bf16[32,1,4,128]{3,0,2,1:T(8,128)(2,1)S(1)}, u32[]{:S(2)}, u32[]{:S(2)}) collective-permute-start(bf16[32,1,4,128]{3,0,2,1:T(8,128)(2,1)S(1)} %get-tuple-element.85), channel_id=1, source_target_pairs={{8,0},{16,8},{24,16},{32,24},{40,32},{48,40},{56,48},{64,56},{72,6... | collective-permute-start | bytes 98312 | tf_op jit(solution)/shard_map/ppermute | solution.py:22
  342.4 8.4 %collective-permute-start.36 = (bf16[32,1,4,128]{3,0,2,1:T(8,128)(2,1)S(1)}, bf16[32,1,4,128]{3,0,2,1:T(8,128)(2,1)S(1)}, u32[]{:S(2)}, u32[]{:S(2)}) collective-permute-start(bf16[32,1,4,128]{3,0,2,1:T(8,128)(2,1)S(1)} %get-tuple-element.76), channel_id=1, source_target_pairs={{0,8},{8,16},{16,24},{24,32},{32,40},{40,48},{48,56},{56,64},{64,7... | collective-permute-start | bytes 98312 | tf_op jit(solution)/shard_map/ppermute | solution.py:20
  348.0 8.4 %collective-permute-start.18 = (bf16[32,6,1,128]{3,0,2,1:T(8,128)(2,1)S(1)}, bf16[32,6,1,128]{3,0,2,1:T(8,128)(2,1)S(1)}, u32[]{:S(2)}, u32[]{:S(2)}) collective-permute-start(bf16[32,6,1,128]{3,0,2,1:T(8,128)(2,1)S(1)} %get-tuple-element.72), channel_id=1, source_target_pairs={{0,1},{1,2},{2,3},{3,4},{4,5},{5,6},{6,7},{8,9},{9,10},{10,11},{11... | collective-permute-start | bytes 147464 | tf_op jit(solution)/shard_map/ppermute | solution.py:20
  349.6 6.9 %collective-permute-start.19 = (bf16[32,6,1,128]{3,0,2,1:T(8,128)(2,1)S(1)}, bf16[32,6,1,128]{3,0,2,1:T(8,128)(2,1)S(1)}, u32[]{:S(2)}, u32[]{:S(2)}) collective-permute-start(bf16[32,6,1,128]{3,0,2,1:T(8,128)(2,1)S(1)} %get-tuple-element.73), channel_id=1, source_target_pairs={{1,0},{2,1},{3,2},{4,3},{5,4},{6,5},{7,6},{9,8},{10,9},{11,10},{12... | collective-permute-start | bytes 147464 | tf_op jit(solution)/shard_map/ppermute | solution.py:22
  351.3 8.8 %collective-permute-start.38 = (bf16[32,6,1,128]{3,0,2,1:T(8,128)(2,1)S(1)}, bf16[32,6,1,128]{3,0,2,1:T(8,128)(2,1)S(1)}, u32[]{:S(2)}, u32[]{:S(2)}) collective-permute-start(bf16[32,6,1,128]{3,0,2,1:T(8,128)(2,1)S(1)} %get-tuple-element.68), channel_id=1, source_target_pairs={{0,1},{1,2},{2,3},{3,4},{4,5},{5,6},{6,7},{8,9},{9,10},{10,11},{11... | collective-permute-start | bytes 147464 | tf_op jit(solution)/shard_map/ppermute | solution.py:20
  (57 other events, 426.3 us)
Sparse Core Ops, SparseCore 0:
  365.3 287.3 all-reduce.13
where the time goes:
time: 666 us; the launch traced here: 664 us
  waiting for transfers between devices  317 us (48%)
  blocking collectives  133 us (20%)
  starting transfers between devices  113 us (17%)
  local copies, waits for them, and re-layouts  38.8 us (6%)
  matrix products  28.7 us (4%)
  other arithmetic  18.4 us (3%)
  between operations  15.8 us (2%)
    psum x1, waiting for transfers between devices, local(): lax.psum((local_in, local_down, local_coarse, local_up, local_out, local_...  286 us
    psum x1, blocking collectives, local(): lax.psum((local_in, local_down, local_coarse, local_up, local_out, local_...  133 us
    ppermute x20, starting transfers between devices, padded_2(): lax.ppermute(tail, axis, [(i, (i + 1) % count) for i in range(ends)])  75.5 us
    ppermute x20, starting transfers between devices, padded_2(): lax.ppermute(head, axis, [((i + 1) % count, i) for i in range(ends)])  37.1 us
    ppermute x20, waiting for transfers between devices, padded_2(): lax.ppermute(head, axis, [((i + 1) % count, i) for i in range(ends)])  30.8 us
    dot_general x90, matrix products, conv_taps(): jnp.einsum('ok,kdhw->odhw', kern[tap_depth, tap_height], window, preferre...  18.8 us
  transfers between devices with their start and end apart: 41, of which 14 were waited for; matrix products, arithmetic and copies ran while one was open for 7% of the time, Pallas kernels for 0%

commit v1 on v0

--- a/solution.py
+++ b/solution.py
@@ -101,6 +101,31 @@
 def silu_grad(value):
     sigma = jax.nn.sigmoid(value)
     return sigma * (1.0 + value * (1.0 - sigma))
+
+
+def reduced(items):
+    sizes = [item.size for item in items]
+    flat = jnp.concatenate([item.reshape(-1) for item in items]).astype(jnp.bfloat16)
+    across = lax.axis_size("height")
+    along = lax.axis_size("depth")
+    rows = -(-flat.size // (across * 128 * 16)) * 16
+    flat = jnp.pad(flat, (0, across * rows * 128 - flat.size))
+    parts = lax.all_to_all(flat.reshape(across, rows, 128), "height", 0, 0)
+    share = jnp.sum(parts.astype(jnp.float32), axis=0).astype(jnp.bfloat16)
+    fine_rows = -(-rows // (along * 8)) * 8
+    share = jnp.pad(share, ((0, along * fine_rows - rows), (0, 0)))
+    parts = lax.all_to_all(share.reshape(along, fine_rows, 128), "depth", 0, 0)
+    own = jnp.sum(parts.astype(jnp.float32), axis=0).astype(jnp.bfloat16)
+    share = lax.all_to_all(jnp.broadcast_to(own, (along, fine_rows, 128)), "depth", 0, 0)
+    share = share.reshape(along * fine_rows, 128)[:rows]
+    total = lax.all_to_all(jnp.broadcast_to(share, (across, rows, 128)), "height", 0, 0)
+    total = total.reshape(-1)
+    out = []
+    at = 0
+    for item, size in zip(items, sizes):
+        out.append(total[at : at + size].reshape(item.shape).astype(jnp.float32))
+        at += size
+    return out
 
 
 def column(vector):
@@ -188,9 +213,8 @@
         for item in (grad_pre1, grad_pre2, grad_pre3, grad_pre4, cotangent)
     ]
     local_biases = jnp.concatenate(parts)
-    summed = lax.psum(
-        (local_in, local_down, local_coarse, local_up, local_out, local_projection, local_biases),
-        ("depth", "height"),
+    summed = reduced(
+        (local_in, local_down, local_coarse, local_up, local_out, local_projection, local_biases)
     )
     grad_in, grad_down, grad_coarse, grad_up, grad_out, grad_projection, grad_biases = [
         item * scale for item in summed

time: 666 us -> 356 us (0.53)
  waiting for transfers between devices: 317 us -> 66.2 us
  blocking collectives: 133 us -> 0 us
  starting transfers between devices: 113 us -> 184 us
  between operations: 15.8 us -> 2.54 us
  local copies, waits for them, and re-layouts: 38.8 us -> 47 us
  matrix products: 28.7 us -> 35.6 us
    psum x1 -> x0, waiting for transfers between devices: 286 us -> none  [local(): lax.psum((local_in, local_down, local_coarse, local_up, local_out, local_...]
    psum x1 -> x0, blocking collectives: 133 us -> none  [local(): lax.psum((local_in, local_down, local_coarse, local_up, local_out, local_...]
    all_to_all x0 -> x4, starting transfers between devices: none -> 68 us  [the longest x1 50 us: reduced(): parts = lax.all_to_all(share.reshape(along, fine_rows, 128), 'depth', 0, 0)]
    all_to_all x0 -> x4, waiting for transfers between devices: none -> 33.7 us  [the longest x1 12.5 us: reduced(): lax.all_to_all(jnp.broadcast_to(own, (along, fine_rows, 128)), 'depth', 0...]
  transfers between devices with their start and end apart: 41 -> 44, of which waited for: 14 -> 15; matrix products, arithmetic and copies ran while one was open for 7% -> 16% of each run, Pallas kernels for 0% -> 0%
where the time goes in v1:
time: 356 us; the launch traced here: 354 us
  starting transfers between devices  184 us (52%)
  waiting for transfers between devices  66.2 us (19%)
  local copies, waits for them, and re-layouts  47 us (13%)
  matrix products  35.6 us (10%)
  other arithmetic  18.5 us (5%)
    ppermute x20, starting transfers between devices, padded_2(): lax.ppermute(tail, axis, [(i, (i + 1) % count) for i in range(ends)])  78.9 us
    all_to_all x1, starting transfers between devices, reduced(): parts = lax.all_to_all(share.reshape(along, fine_rows, 128), 'depth', 0, 0)  50 us
    ppermute x20, starting transfers between devices, padded_2(): lax.ppermute(head, axis, [((i + 1) % count, i) for i in range(ends)])  37.1 us
    ppermute x20, waiting for transfers between devices, padded_2(): lax.ppermute(head, axis, [((i + 1) % count, i) for i in range(ends)])  32.5 us
    dot_general x90, matrix products, conv_taps(): jnp.einsum('ok,kdhw->odhw', kern[tap_depth, tap_height], window, preferre...  20.3 us
    dot_general x45, matrix products, kernel_taps(): jnp.einsum('odhw,kdhw->ok', grad, window, preferred_element_type=jnp.floa...  14.1 us
    all_to_all x1, waiting for transfers between devices, reduced(): lax.all_to_all(jnp.broadcast_to(own, (along, fine_rows, 128)), 'depth', 0...  12.5 us
    all_to_all x1, waiting for transfers between devices, reduced(): parts = lax.all_to_all(share.reshape(along, fine_rows, 128), 'depth', 0, 0)  12.4 us
  transfers between devices with their start and end apart: 44, of which 15 were waited for; matrix products, arithmetic and copies ran while one was open for 16% of the time, Pallas kernels for 0%

profile of v1, /device:TPU:1, one launch (start us, length us, event | category | flops | bytes accessed | tf_op | source)
XLA Modules:
  0.0 354.0 jit_solution(4077684414645469433)
XLA Ops:
  1.5 4.6 %collective-permute-start = (bf16[32,1,4,128]{3,0,2,1:T(8,128)(2,1)S(1)}, bf16[32,1,4,128]{3,0,2,1:T(8,128)(2,1)S(1)}, u32[]{:S(2)}, u32[]{:S(2)}) collective-permute-start(bf16[32,1,4,128]{3,0,2,1:T(8,128)(2,1)S(1)} %copy.397), channel_id=1, source_target_pairs={{0,8},{8,16},{16,24},{24,32},{32,40},{40,48},{48,56},{56,64},{64,7... | collective-permute-start | bytes 98312 | tf_op jit(solution)/shard_map/ppermute | solution.py:20
  6.2 5.5 %collective-permute-start.1 = (bf16[32,1,4,128]{3,0,2,1:T(8,128)(2,1)S(1)}, bf16[32,1,4,128]{3,0,2,1:T(8,128)(2,1)S(1)}, u32[]{:S(2)}, u32[]{:S(2)}) collective-permute-start(bf16[32,1,4,128]{3,0,2,1:T(8,128)(2,1)S(1)} %copy.398), channel_id=1, source_target_pairs={{8,0},{16,8},{24,16},{32,24},{40,32},{48,40},{56,48},{64,56},{72,6... | collective-permute-start | bytes 98312 | tf_op jit(solution)/shard_map/ppermute | solution.py:22
  42.8 4.0 %collective-permute-start.22 = (bf16[32,6,1,128]{3,0,2,1:T(8,128)(2,1)}, bf16[32,6,1,128]{3,0,2,1:T(8,128)(2,1)S(1)}, u32[]{:S(2)}, u32[]{:S(2)}) collective-permute-start(bf16[32,6,1,128]{3,0,2,1:T(8,128)(2,1)} %get-tuple-element.75), channel_id=1, source_target_pairs={{0,1},{1,2},{2,3},{3,4},{4,5},{5,6},{6,7},{8,9},{9,10},{10,11},{11... | collective-permute-start | bytes 147464 | tf_op jit(solution)/shard_map/ppermute | solution.py:20
  60.8 4.3 %collective-permute-start.6 = (bf16[32,4,1,64]{0,3,2,1:T(8,128)(2,1)S(1)}, bf16[32,4,1,64]{0,3,2,1:T(8,128)(2,1)S(1)}, u32[]{:S(2)}, u32[]{:S(2)}) collective-permute-start(bf16[32,4,1,64]{0,3,2,1:T(8,128)(2,1)S(1)} %get-tuple-element.93), channel_id=1, source_target_pairs={{0,1},{1,2},{2,3},{3,4},{4,5},{5,6},{6,7},{8,9},{9,10},{10,11},{11... | collective-permute-start | bytes 49160 | tf_op jit(solution)/shard_map/ppermute | solution.py:20
  72.8 3.8 %collective-permute-start.8 = (bf16[64,1,1,32]{0,3,2,1:T(8,128)(2,1)S(1)}, bf16[64,1,1,32]{0,3,2,1:T(8,128)(2,1)S(1)}, u32[]{:S(2)}, u32[]{:S(2)}) collective-permute-start(bf16[64,1,1,32]{0,3,2,1:T(8,128)(2,1)S(1)} %fusion.209), channel_id=1, source_target_pairs={{0,8},{8,16},{16,24},{24,32},{32,40},{40,48},{48,56},{56,64},{64,7... | collective-permute-start | bytes 12296 | tf_op jit(solution)/shard_map/ppermute | solution.py:20
  81.6 4.4 %collective-permute-start.10 = (bf16[64,3,1,32]{0,3,2,1:T(8,128)(2,1)S(1)}, bf16[64,3,1,32]{0,3,2,1:T(8,128)(2,1)S(1)}, u32[]{:S(2)}, u32[]{:S(2)}) collective-permute-start(bf16[64,3,1,32]{0,3,2,1:T(8,128)(2,1)S(1)} %pad_maximum_fusion.25), channel_id=1, source_target_pairs={{0,1},{1,2},{2,3},{3,4},{4,5},{5,6},{6,7},{8,9},{9,10},{10,11},{11... | collective-permute-start | bytes 36872 | tf_op jit(solution)/shard_map/ppermute | solution.py:20
  88.2 4.8 %collective-permute-done.11 = bf16[64,3,1,32]{0,3,2,1:T(8,128)(2,1)S(1)} collective-permute-done((bf16[64,3,1,32]{0,3,2,1:T(8,128)(2,1)S(1)}, bf16[64,3,1,32]{0,3,2,1:T(8,128)(2,1)S(1)}, u32[]{:S(2)}, u32[]{:S(2)}) %collective-permute-start.11) | collective-permute-done | bytes 12320 | tf_op jit(solution)/shard_map/ppermute | solution.py:22
  103.5 6.7 %collective-permute-start.14 = (bf16[64,4,1,64]{0,3,2,1:T(8,128)(2,1)}, bf16[64,4,1,64]{0,3,2,1:T(8,128)(2,1)}, u32[]{:S(2)}, u32[]{:S(2)}) collective-permute-start(bf16[64,4,1,64]{0,3,2,1:T(8,128)(2,1)} %get-tuple-element.91), channel_id=1, source_target_pairs={{0,1},{1,2},{2,3},{3,4},{4,5},{5,6},{6,7},{8,9},{9,10},{10,11},{11... | collective-permute-start | bytes 98312 | tf_op jit(solution)/shard_map/ppermute | solution.py:20
  130.4 4.0 %collective-permute-start.16 = (bf16[32,1,4,128]{3,0,2,1:T(8,128)(2,1)S(1)}, bf16[32,1,4,128]{3,0,2,1:T(8,128)(2,1)S(1)}, u32[]{:S(2)}, u32[]{:S(2)}) collective-permute-start(bf16[32,1,4,128]{3,0,2,1:T(8,128)(2,1)S(1)} %get-tuple-element.89), channel_id=1, source_target_pairs={{0,8},{8,16},{16,24},{24,32},{32,40},{40,48},{48,56},{56,64},{64,7... | collective-permute-start | bytes 98312 | tf_op jit(solution)/shard_map/ppermute | solution.py:20
  151.1 4.3 %collective-permute-start.18 = (bf16[32,6,1,128]{3,0,2,1:T(8,128)(2,1)}, bf16[32,6,1,128]{3,0,2,1:T(8,128)(2,1)S(1)}, u32[]{:S(2)}, u32[]{:S(2)}) collective-permute-start(bf16[32,6,1,128]{3,0,2,1:T(8,128)(2,1)} %get-tuple-element.77), channel_id=1, source_target_pairs={{0,1},{1,2},{2,3},{3,4},{4,5},{5,6},{6,7},{8,9},{9,10},{10,11},{11... | collective-permute-start | bytes 147464 | tf_op jit(solution)/shard_map/ppermute | solution.py:20
  161.1 4.3 %collective-permute-start.28 = (bf16[64,1,1,32]{0,3,2,1:T(8,128)(2,1)S(1)}, bf16[64,1,1,32]{0,3,2,1:T(8,128)(2,1)S(1)}, u32[]{:S(2)}, u32[]{:S(2)}) collective-permute-start(bf16[64,1,1,32]{0,3,2,1:T(8,128)(2,1)S(1)} %bitcast.1259), channel_id=1, source_target_pairs={{0,8},{8,16},{16,24},{24,32},{32,40},{40,48},{48,56},{56,64},{64,7... | collective-permute-start | bytes 12296 | tf_op jit(solution)/shard_map/ppermute | solution.py:20
  170.4 4.4 %collective-permute-start.30 = (bf16[64,3,1,32]{0,3,2,1:T(8,128)(2,1)S(1)}, bf16[64,3,1,32]{0,3,2,1:T(8,128)(2,1)S(1)}, u32[]{:S(2)}, u32[]{:S(2)}) collective-permute-start(bf16[64,3,1,32]{0,3,2,1:T(8,128)(2,1)S(1)} %pad_maximum_fusion.26), channel_id=1, source_target_pairs={{0,1},{1,2},{2,3},{3,4},{4,5},{5,6},{6,7},{8,9},{9,10},{10,11},{11... | collective-permute-start | bytes 36872 | tf_op jit(solution)/shard_map/ppermute | solution.py:20
  184.5 4.6 %collective-permute-start.32 = (bf16[64,1,2,64]{0,3,2,1:T(8,128)(2,1)S(1)}, bf16[64,1,2,64]{0,3,2,1:T(8,128)(2,1)S(1)}, u32[]{:S(2)}, u32[]{:S(2)}) collective-permute-start(bf16[64,1,2,64]{0,3,2,1:T(8,128)(2,1)S(1)} %get-tuple-element.101), channel_id=1, source_target_pairs={{0,8},{8,16},{16,24},{24,32},{32,40},{40,48},{48,56},{56,64},{64,7... | collective-permute-start | bytes 49160 | tf_op jit(solution)/shard_map/ppermute | solution.py:20
  195.5 4.4 %collective-permute-start.34 = (bf16[64,4,1,64]{0,3,2,1:T(8,128)(2,1)S(1)}, bf16[64,4,1,64]{0,3,2,1:T(8,128)(2,1)S(1)}, u32[]{:S(2)}, u32[]{:S(2)}) collective-permute-start(bf16[64,4,1,64]{0,3,2,1:T(8,128)(2,1)S(1)} %get-tuple-element.83), channel_id=1, source_target_pairs={{0,1},{1,2},{2,3},{3,4},{4,5},{5,6},{6,7},{8,9},{9,10},{10,11},{11... | collective-permute-start | bytes 98312 | tf_op jit(solution)/shard_map/ppermute | solution.py:20
  202.2 5.1 %collective-permute-done.35 = bf16[64,4,1,64]{0,3,2,1:T(8,128)(2,1)S(1)} collective-permute-done((bf16[64,4,1,64]{0,3,2,1:T(8,128)(2,1)S(1)}, bf16[64,4,1,64]{0,3,2,1:T(8,128)(2,1)S(1)}, u32[]{:S(2)}, u32[]{:S(2)}) %collective-permute-start.35) | collective-permute-done | bytes 32800 | tf_op jit(solution)/shard_map/ppermute | solution.py:22
  216.3 3.7 %concatenate.129 = bf16[334080]{0:T(1024)(128)(2,1)S(1)} concatenate(bf16[27648]{0:T(1024)(128)(2,1)S(1)} %reshape.306, bf16[55296]{0:T(1024)(128)(2,1)S(1)} %copy-done.9, bf16[110592]{0:T(1024)(128)(2,1)S(1)} %copy-done.7, bf16[110592]{0:T(1024)(128)(2,1)S(1)} %copy-done.6, bf16[27648]{0:T(1024)(128)(2,1)S(1)} %copy-done.21, bf16[2048]{0:T(1024)(128)(2,1)S(1)} %copy-done.26, ...), dimensions={0} | concatenate | bytes 1336320 | tf_op jit(solution)/shard_map/concatenate | solution.py:108
  220.9 7.8 %all-to-all-start = ((bf16[8,336,128]{2,1,0:T(8,128)(2,1)}), bf16[8,336,128]{2,1,0:T(8,128)(2,1)S(1)}, u32[]{:S(2)}, u32[]{:S(2)}) async-start(bf16[8,336,128]{2,1,0:T(8,128)(2,1)} %bitcast.427), calls=%async_computation | async-start | bytes 1376256 | tf_op jit(solution)/shard_map/all_to_all | solution.py:113
  228.8 5.1 %collective-permute-start.36 = (bf16[32,1,4,128]{3,0,2,1:T(8,128)(2,1)S(1)}, bf16[32,1,4,128]{3,0,2,1:T(8,128)(2,1)S(1)}, u32[]{:S(2)}, u32[]{:S(2)}) collective-permute-start(bf16[32,1,4,128]{3,0,2,1:T(8,128)(2,1)S(1)} %get-tuple-element.81), channel_id=1, source_target_pairs={{0,8},{8,16},{16,24},{24,32},{32,40},{40,48},{48,56},{56,64},{64,7... | collective-permute-start | bytes 98312 | tf_op jit(solution)/shard_map/ppermute | solution.py:20
  249.0 50.0 %all-to-all-start.1 = ((bf16[64,8,128]{2,1,0:T(8,128)(2,1)}), bf16[64,8,128]{2,1,0:T(8,128)(2,1)S(1)}, u32[]{:S(2)}, u32[]{:S(2)}) async-start(bf16[64,8,128]{2,1,0:T(8,128)(2,1)} %pad_bitcast_fusion), calls=%async_computation.1 | async-start | bytes 262144 | tf_op jit(solution)/shard_map/all_to_all | solution.py:117
  299.4 12.4 %all-to-all-done.1 = bf16[64,8,128]{2,1,0:T(8,128)(2,1)S(1)} async-done(((bf16[64,8,128]{2,1,0:T(8,128)(2,1)}), bf16[64,8,128]{2,1,0:T(8,128)(2,1)S(1)}, u32[]{:S(2)}, u32[]{:S(2)}) %all-to-all-start.1) | async-done | bytes 131104 | tf_op jit(solution)/shard_map/all_to_all | solution.py:117
  312.5 4.4 %all-to-all-start.2 = ((bf16[64,8,128]{2,1,0:T(8,128)(2,1)}), bf16[64,8,128]{2,1,0:T(8,128)(2,1)S(1)}, u32[]{:S(2)}, u32[]{:S(2)}) async-start(bf16[64,8,128]{2,1,0:T(8,128)(2,1)} %broadcast_in_dim.22), calls=%async_computation.2 | async-start | bytes 262144 | tf_op jit(solution)/shard_map/all_to_all | solution.py:119
  317.3 12.5 %all-to-all-done.2 = bf16[64,8,128]{2,1,0:T(8,128)(2,1)S(1)} async-done(((bf16[64,8,128]{2,1,0:T(8,128)(2,1)}), bf16[64,8,128]{2,1,0:T(8,128)(2,1)S(1)}, u32[]{:S(2)}, u32[]{:S(2)}) %all-to-all-start.2) | async-done | bytes 131104 | tf_op jit(solution)/shard_map/all_to_all | solution.py:119
  330.8 5.8 %all-to-all-start.3 = ((bf16[8,336,128]{2,1,0:T(8,128)(2,1)}), bf16[8,336,128]{2,1,0:T(8,128)(2,1)S(1)}, u32[]{:S(2)}, u32[]{:S(2)}) async-start(bf16[8,336,128]{2,1,0:T(8,128)(2,1)} %broadcast_in_dim.46), calls=%async_computation.3 | async-start | bytes 1376256 | tf_op jit(solution)/shard_map/all_to_all | solution.py:121
  338.3 8.8 %all-to-all-done.3 = bf16[8,336,128]{2,1,0:T(8,128)(2,1)S(1)} async-done(((bf16[8,336,128]{2,1,0:T(8,128)(2,1)}), bf16[8,336,128]{2,1,0:T(8,128)(2,1)S(1)}, u32[]{:S(2)}, u32[]{:S(2)}) %all-to-all-start.3) | async-done | bytes 688160 | tf_op jit(solution)/shard_map/all_to_all | solution.py:121
  (416 shorter events, 172.1 us)
Async XLA Ops:
  1.5 37.0 %collective-permute-start = (bf16[32,1,4,128]{3,0,2,1:T(8,128)(2,1)S(1)}, bf16[32,1,4,128]{3,0,2,1:T(8,128)(2,1)S(1)}, u32[]{:S(2)}, u32[]{:S(2)}) collective-permute-start(bf16[32,1,4,128]{3,0,2,1:T(8,128)(2,1)S(1)} %copy.397), channel_id=1, source_target_pairs={{0,8},{8,16},{16,24},{24,32},{32,40},{40,48},{48,56},{56,64},{64,7... | collective-permute-start | bytes 98312 | tf_op jit(solution)/shard_map/ppermute | solution.py:20
  6.2 32.5 %collective-permute-start.1 = (bf16[32,1,4,128]{3,0,2,1:T(8,128)(2,1)S(1)}, bf16[32,1,4,128]{3,0,2,1:T(8,128)(2,1)S(1)}, u32[]{:S(2)}, u32[]{:S(2)}) collective-permute-start(bf16[32,1,4,128]{3,0,2,1:T(8,128)(2,1)S(1)} %copy.398), channel_id=1, source_target_pairs={{8,0},{16,8},{24,16},{32,24},{40,32},{48,40},{56,48},{64,56},{72,6... | collective-permute-start | bytes 98312 | tf_op jit(solution)/shard_map/ppermute | solution.py:22
  12.5 28.8 %collective-permute-start.20 = (bf16[32,1,4,128]{3,0,2,1:T(8,128)(2,1)S(1)}, bf16[32,1,4,128]{3,0,2,1:T(8,128)(2,1)}, u32[]{:S(2)}, u32[]{:S(2)}) collective-permute-start(bf16[32,1,4,128]{3,0,2,1:T(8,128)(2,1)S(1)} %copy.399), channel_id=1, source_target_pairs={{0,8},{8,16},{16,24},{24,32},{32,40},{40,48},{48,56},{56,64},{64,7... | collective-permute-start | bytes 98312 | tf_op jit(solution)/shard_map/ppermute | solution.py:20
  14.4 27.7 %collective-permute-start.21 = (bf16[32,1,4,128]{3,0,2,1:T(8,128)(2,1)S(1)}, bf16[32,1,4,128]{3,0,2,1:T(8,128)(2,1)S(1)}, u32[]{:S(2)}, u32[]{:S(2)}) collective-permute-start(bf16[32,1,4,128]{3,0,2,1:T(8,128)(2,1)S(1)} %copy.400), channel_id=1, source_target_pairs={{8,0},{16,8},{24,16},{32,24},{40,32},{48,40},{56,48},{64,56},{72,6... | collective-permute-start | bytes 98312 | tf_op jit(solution)/shard_map/ppermute | solution.py:22
  38.7 9.4 %collective-permute-start.2 = (bf16[32,6,1,128]{3,0,2,1:T(8,128)(2,1)S(1)}, bf16[32,6,1,128]{3,0,2,1:T(8,128)(2,1)S(1)}, u32[]{:S(2)}, u32[]{:S(2)}) collective-permute-start(bf16[32,6,1,128]{3,0,2,1:T(8,128)(2,1)S(1)} %get-tuple-element.79), channel_id=1, source_target_pairs={{0,1},{1,2},{2,3},{3,4},{4,5},{5,6},{6,7},{8,9},{9,10},{10,11},{11... | collective-permute-start | bytes 147464 | tf_op jit(solution)/shard_map/ppermute | solution.py:20
  40.0 8.1 %collective-permute-start.3 = (bf16[32,6,1,128]{3,0,2,1:T(8,128)(2,1)S(1)}, bf16[32,6,1,128]{3,0,2,1:T(8,128)(2,1)S(1)}, u32[]{:S(2)}, u32[]{:S(2)}) collective-permute-start(bf16[32,6,1,128]{3,0,2,1:T(8,128)(2,1)S(1)} %get-tuple-element.80), channel_id=1, source_target_pairs={{1,0},{2,1},{3,2},{4,3},{5,4},{6,5},{7,6},{9,8},{10,9},{11,10},{12... | collective-permute-start | bytes 147464 | tf_op jit(solution)/shard_map/ppermute | solution.py:22
  42.8 14.6 %collective-permute-start.22 = (bf16[32,6,1,128]{3,0,2,1:T(8,128)(2,1)}, bf16[32,6,1,128]{3,0,2,1:T(8,128)(2,1)S(1)}, u32[]{:S(2)}, u32[]{:S(2)}) collective-permute-start(bf16[32,6,1,128]{3,0,2,1:T(8,128)(2,1)} %get-tuple-element.75), channel_id=1, source_target_pairs={{0,1},{1,2},{2,3},{3,4},{4,5},{5,6},{6,7},{8,9},{9,10},{10,11},{11... | collective-permute-start | bytes 147464 | tf_op jit(solution)/shard_map/ppermute | solution.py:20
  46.8 10.7 %collective-permute-start.23 = (bf16[32,6,1,128]{3,0,2,1:T(8,128)(2,1)}, bf16[32,6,1,128]{3,0,2,1:T(8,128)(2,1)S(1)}, u32[]{:S(2)}, u32[]{:S(2)}) collective-permute-start(bf16[32,6,1,128]{3,0,2,1:T(8,128)(2,1)} %get-tuple-element.76), channel_id=1, source_target_pairs={{1,0},{2,1},{3,2},{4,3},{5,4},{6,5},{7,6},{9,8},{10,9},{11,10},{12... | collective-permute-start | bytes 147464 | tf_op jit(solution)/shard_map/ppermute | solution.py:22
  86.0 7.0 %collective-permute-start.11 = (bf16[64,3,1,32]{0,3,2,1:T(8,128)(2,1)S(1)}, bf16[64,3,1,32]{0,3,2,1:T(8,128)(2,1)S(1)}, u32[]{:S(2)}, u32[]{:S(2)}) collective-permute-start(bf16[64,3,1,32]{0,3,2,1:T(8,128)(2,1)S(1)} %pad_maximum_fusion.25), channel_id=1, source_target_pairs={{1,0},{2,1},{3,2},{4,3},{5,4},{6,5},{7,6},{9,8},{10,9},{11,10},{12... | collective-permute-start | bytes 36872 | tf_op jit(solution)/shard_map/ppermute | solution.py:22
  103.5 10.1 %collective-permute-start.14 = (bf16[64,4,1,64]{0,3,2,1:T(8,128)(2,1)}, bf16[64,4,1,64]{0,3,2,1:T(8,128)(2,1)}, u32[]{:S(2)}, u32[]{:S(2)}) collective-permute-start(bf16[64,4,1,64]{0,3,2,1:T(8,128)(2,1)} %get-tuple-element.91), channel_id=1, source_target_pairs={{0,1},{1,2},{2,3},{3,4},{4,5},{5,6},{6,7},{8,9},{9,10},{10,11},{11... | collective-permute-start | bytes 98312 | tf_op jit(solution)/shard_map/ppermute | solution.py:20
  130.4 20.1 %collective-permute-start.16 = (bf16[32,1,4,128]{3,0,2,1:T(8,128)(2,1)S(1)}, bf16[32,1,4,128]{3,0,2,1:T(8,128)(2,1)S(1)}, u32[]{:S(2)}, u32[]{:S(2)}) collective-permute-start(bf16[32,1,4,128]{3,0,2,1:T(8,128)(2,1)S(1)} %get-tuple-element.89), channel_id=1, source_target_pairs={{0,8},{8,16},{16,24},{24,32},{32,40},{40,48},{48,56},{56,64},{64,7... | collective-permute-start | bytes 98312 | tf_op jit(solution)/shard_map/ppermute | solution.py:20
  134.4 16.1 %collective-permute-start.17 = (bf16[32,1,4,128]{3,0,2,1:T(8,128)(2,1)S(1)}, bf16[32,1,4,128]{3,0,2,1:T(8,128)(2,1)S(1)}, u32[]{:S(2)}, u32[]{:S(2)}) collective-permute-start(bf16[32,1,4,128]{3,0,2,1:T(8,128)(2,1)S(1)} %get-tuple-element.90), channel_id=1, source_target_pairs={{8,0},{16,8},{24,16},{32,24},{40,32},{48,40},{56,48},{64,56},{72,6... | collective-permute-start | bytes 98312 | tf_op jit(solution)/shard_map/ppermute | solution.py:22
  136.3 9.2 %collective-permute-start.24 = (bf16[64,1,2,64]{0,3,2,1:T(8,128)(2,1)}, bf16[64,1,2,64]{0,3,2,1:T(8,128)(2,1)S(1)}, u32[]{:S(2)}, u32[]{:S(2)}) collective-permute-start(bf16[64,1,2,64]{0,3,2,1:T(8,128)(2,1)} %get-tuple-element.103), channel_id=1, source_target_pairs={{0,8},{8,16},{16,24},{24,32},{32,40},{40,48},{48,56},{56,64},{64,7... | collective-permute-start | bytes 49160 | tf_op jit(solution)/shard_map/ppermute | solution.py:20
  145.8 10.8 %collective-permute-start.26 = (bf16[64,4,1,64]{0,3,2,1:T(8,128)(2,1)S(1)}, bf16[64,4,1,64]{0,3,2,1:T(8,128)(2,1)S(1)}, u32[]{:S(2)}, u32[]{:S(2)}) collective-permute-start(bf16[64,4,1,64]{0,3,2,1:T(8,128)(2,1)S(1)} %get-tuple-element.85), channel_id=1, source_target_pairs={{0,1},{1,2},{2,3},{3,4},{4,5},{5,6},{6,7},{8,9},{9,10},{10,11},{11... | collective-permute-start | bytes 98312 | tf_op jit(solution)/shard_map/ppermute | solution.py:20
  149.1 7.5 %collective-permute-start.27 = (bf16[64,4,1,64]{0,3,2,1:T(8,128)(2,1)S(1)}, bf16[64,4,1,64]{0,3,2,1:T(8,128)(2,1)S(1)}, u32[]{:S(2)}, u32[]{:S(2)}) collective-permute-start(bf16[64,4,1,64]{0,3,2,1:T(8,128)(2,1)S(1)} %get-tuple-element.86), channel_id=1, source_target_pairs={{1,0},{2,1},{3,2},{4,3},{5,4},{6,5},{7,6},{9,8},{10,9},{11,10},{12... | collective-permute-start | bytes 98312 | tf_op jit(solution)/shard_map/ppermute | solution.py:22
  151.1 39.9 %collective-permute-start.18 = (bf16[32,6,1,128]{3,0,2,1:T(8,128)(2,1)}, bf16[32,6,1,128]{3,0,2,1:T(8,128)(2,1)S(1)}, u32[]{:S(2)}, u32[]{:S(2)}) collective-permute-start(bf16[32,6,1,128]{3,0,2,1:T(8,128)(2,1)} %get-tuple-element.77), channel_id=1, source_target_pairs={{0,1},{1,2},{2,3},{3,4},{4,5},{5,6},{6,7},{8,9},{9,10},{10,11},{11... | collective-permute-start | bytes 147464 | tf_op jit(solution)/shard_map/ppermute | solution.py:20
  155.3 35.7 %collective-permute-start.19 = (bf16[32,6,1,128]{3,0,2,1:T(8,128)(2,1)}, bf16[32,6,1,128]{3,0,2,1:T(8,128)(2,1)S(1)}, u32[]{:S(2)}, u32[]{:S(2)}) collective-permute-start(bf16[32,6,1,128]{3,0,2,1:T(8,128)(2,1)} %get-tuple-element.78), channel_id=1, source_target_pairs={{1,0},{2,1},{3,2},{4,3},{5,4},{6,5},{7,6},{9,8},{10,9},{11,10},{12... | collective-permute-start | bytes 147464 | tf_op jit(solution)/shard_map/ppermute | solution.py:22
  184.5 10.9 %collective-permute-start.32 = (bf16[64,1,2,64]{0,3,2,1:T(8,128)(2,1)S(1)}, bf16[64,1,2,64]{0,3,2,1:T(8,128)(2,1)S(1)}, u32[]{:S(2)}, u32[]{:S(2)}) collective-permute-start(bf16[64,1,2,64]{0,3,2,1:T(8,128)(2,1)S(1)} %get-tuple-element.101), channel_id=1, source_target_pairs={{0,8},{8,16},{16,24},{24,32},{32,40},{40,48},{48,56},{56,64},{64,7... | collective-permute-start | bytes 49160 | tf_op jit(solution)/shard_map/ppermute | solution.py:20
  199.8 7.4 %collective-permute-start.35 = (bf16[64,4,1,64]{0,3,2,1:T(8,128)(2,1)S(1)}, bf16[64,4,1,64]{0,3,2,1:T(8,128)(2,1)S(1)}, u32[]{:S(2)}, u32[]{:S(2)}) collective-permute-start(bf16[64,4,1,64]{0,3,2,1:T(8,128)(2,1)S(1)} %get-tuple-element.84), channel_id=1, source_target_pairs={{1,0},{2,1},{3,2},{4,3},{5,4},{6,5},{7,6},{9,8},{10,9},{11,10},{12... | collective-permute-start | bytes 98312 | tf_op jit(solution)/shard_map/ppermute | solution.py:22
  220.9 27.2 %all-to-all-start = ((bf16[8,336,128]{2,1,0:T(8,128)(2,1)}), bf16[8,336,128]{2,1,0:T(8,128)(2,1)S(1)}, u32[]{:S(2)}, u32[]{:S(2)}) async-start(bf16[8,336,128]{2,1,0:T(8,128)(2,1)} %bitcast.427), calls=%async_computation | async-start | bytes 1376256 | tf_op jit(solution)/shard_map/all_to_all | solution.py:113
  228.8 7.2 %collective-permute-start.36 = (bf16[32,1,4,128]{3,0,2,1:T(8,128)(2,1)S(1)}, bf16[32,1,4,128]{3,0,2,1:T(8,128)(2,1)S(1)}, u32[]{:S(2)}, u32[]{:S(2)}) collective-permute-start(bf16[32,1,4,128]{3,0,2,1:T(8,128)(2,1)S(1)} %get-tuple-element.81), channel_id=1, source_target_pairs={{0,8},{8,16},{16,24},{24,32},{32,40},{40,48},{48,56},{56,64},{64,7... | collective-permute-start | bytes 98312 | tf_op jit(solution)/shard_map/ppermute | solution.py:20
  249.0 62.8 %all-to-all-start.1 = ((bf16[64,8,128]{2,1,0:T(8,128)(2,1)}), bf16[64,8,128]{2,1,0:T(8,128)(2,1)S(1)}, u32[]{:S(2)}, u32[]{:S(2)}) async-start(bf16[64,8,128]{2,1,0:T(8,128)(2,1)} %pad_bitcast_fusion), calls=%async_computation.1 | async-start | bytes 262144 | tf_op jit(solution)/shard_map/all_to_all | solution.py:117
  312.5 17.3 %all-to-all-start.2 = ((bf16[64,8,128]{2,1,0:T(8,128)(2,1)}), bf16[64,8,128]{2,1,0:T(8,128)(2,1)S(1)}, u32[]{:S(2)}, u32[]{:S(2)}) async-start(bf16[64,8,128]{2,1,0:T(8,128)(2,1)} %broadcast_in_dim.22), calls=%async_computation.2 | async-start | bytes 262144 | tf_op jit(solution)/shard_map/all_to_all | solution.py:119
  330.8 16.2 %all-to-all-start.3 = ((bf16[8,336,128]{2,1,0:T(8,128)(2,1)}), bf16[8,336,128]{2,1,0:T(8,128)(2,1)S(1)}, u32[]{:S(2)}, u32[]{:S(2)}) async-start(bf16[8,336,128]{2,1,0:T(8,128)(2,1)} %broadcast_in_dim.46), calls=%async_computation.3 | async-start | bytes 1376256 | tf_op jit(solution)/shard_map/all_to_all | solution.py:121
  (53 other events, 573.6 us)

commit v2 on v1

v2 whole, which is shorter than its diff:
```python
import functools
import math

import jax
import jax.numpy as jnp
from jax import lax
from jax.experimental import pallas as pl
from jax.experimental.pallas import tpu as pltpu
from jax.sharding import PartitionSpec as P

CH_FINE = 32
CH_MID = 64
FINE_W = 128
MID_W = 64
COARSE_W = 32
BF = jnp.bfloat16
F32 = jnp.float32


def mm(a, b):
    return lax.dot_general(a, b, (((1,), (0,)), ((), ())), preferred_element_type=F32)


def mm_nt(a, b):
    return lax.dot_general(a, b, (((1,), (1,)), ((), ())), preferred_element_type=F32)


def iota(shape, dim):
    return lax.broadcasted_iota(jnp.int32, shape, dim)


def shifted(x, rows, cells, width):
    if rows == 0 and cells == 0:
        return x
    lanes = x.shape[1]
    step = rows * width + cells
    y = pltpu.roll(x, (-step) % lanes, 1)
    lane = iota((1, lanes), 1)
    keep = None
    if cells:
        cell = lax.rem(lane, width) + cells
        keep = (cell >= 0) & (cell < width)
    if rows:
        at = lane + rows * width
        inside = (at >= 0) & (at < lanes)
        keep = inside if keep is None else keep & inside
    return jnp.where(keep, y, 0.0)


def widened(plane, width):
    wide = plane.astype(F32)
    return jnp.concatenate(
        [shifted(wide, 0, -1, width).astype(BF), plane, shifted(wide, 0, 1, width).astype(BF)], axis=0
    )


def row_taps(plane, width):
    wide = plane.astype(F32)
    return jnp.concatenate(
        [shifted(wide, 1, 0, width).astype(BF), plane, shifted(wide, -1, 0, width).astype(BF)], axis=0
    )


def fold_cells(taps, width):
    ins = taps.shape[0] // 3
    return (
        shifted(taps[:ins], 0, 1, width)
        + taps[ins : 2 * ins]
        + shifted(taps[2 * ins :], 0, -1, width)
    )


def turned(kern):
    side = kern.shape[1]
    eye = (iota((side, side), 0) == iota((side, side), 1)).astype(F32).astype(BF)
    return mm_nt(eye, kern).astype(BF)


def gate(v):
    return 1.0 / (1.0 + jnp.exp(-v))


def split(v):
    high = v.astype(BF)
    return high, (v - high.astype(F32)).astype(BF)


def pool_matrix(lanes, width):
    r = iota((lanes, lanes // 4), 0)
    q = iota((lanes, lanes // 4), 1)
    goal = (r // (2 * width)) * (width // 2) + lax.rem(r, width) // 2
    return (goal == q).astype(F32).astype(BF)


def spread_matrix(lanes, width):
    r = iota((lanes // 4, lanes), 1)
    q = iota((lanes // 4, lanes), 0)
    goal = (r // (2 * width)) * (width // 2) + lax.rem(r, width) // 2
    return (goal == q).astype(F32).astype(BF)


def window_spread():
    r = iota((6 * MID_W, 6 * FINE_W), 0)
    q = iota((6 * MID_W, 6 * FINE_W), 1)
    row = (q // FINE_W + 1) // 2 + 1
    hit = (r // MID_W == row) & (lax.rem(r, MID_W) == lax.rem(q, FINE_W) // 2)
    return hit.astype(F32).astype(BF)


def window(pad_ref, place, at):
    return pad_ref[place, :, pl.ds(pl.multiple_of(128 * at, 128), 384)]


def fill_padded(pad_ref, place, plane):
    chans, lanes = plane.shape
    pad_ref[place, :, 0:128] = jnp.zeros((chans, 128), plane.dtype)
    pad_ref[place, :, 128 : 128 + lanes] = plane
    pad_ref[place, :, 128 + lanes : 256 + lanes] = jnp.zeros((chans, 128), plane.dtype)


def tap_windows(win):
    wide = win.astype(F32)
    cells = [shifted(wide, 0, c - 1, MID_W) for c in range(3)]
    out = []
    for b in range(3):
        start = 128 + (b - 1) * MID_W
        out.append(jnp.concatenate([v[:, start : start + 128] for v in cells], axis=0).astype(BF))
    return out


def gathered(g_ref, place, low, high):
    return jnp.concatenate([g_ref[h, place, low:high, :] for h in range(g_ref.shape[0])], axis=1)


def fine_kernel(nd, nh, idx, xl, xc, xr, kin, kout, bias, act, ds1, gsk, fx, cot, mid, planes, pre, full, gfull, kt):
    dep, hei = idx[0], idx[1]
    for d in range(10):
        src, i = (xl, d) if d < 3 else (xc, d - 3) if d < 7 else (xr, d - 7)
        planes[d] = jnp.concatenate([src[i, h] for h in range(8)], axis=1)
    kt[...] = turned(kout[...])
    pre[...] = jnp.zeros_like(pre)

    def forward(d, carry):
        y = mm(kin[...], widened(planes[d, 0:32, :], FINE_W))
        for a in range(3):
            part = y[96 * a : 96 * a + 32, 0:768]
            for b in (1, 2):
                part += y[96 * a + 32 * b : 96 * a + 32 * b + 32, 128 * b : 128 * b + 768]
            pre[d - a + 2] += part
        return carry

    lax.fori_loop(0, 10, forward, 0)
    h_at = iota((1, 768), 1) // FINE_W - 1 + 4 * hei
    h_in = (h_at >= 0) & (h_at < 4 * nh)

    def finish(d, carry):
        at = 4 * dep + d - 2
        inside = h_in & (at >= 0) & (at < 4 * nd)
        v = pre[d + 2] + bias[...]
        s = gate(v)
        full[d] = jnp.where(inside, v * s, 0.0).astype(BF)
        pre[d + 2] = jnp.where(inside, s * (1.0 + v * (1.0 - s)), 0.0)
        stack = jnp.concatenate(
            [
                planes[d + 2 - a, 32:64, 128 * (2 - b) : 128 * (2 - b) + 768]
                for a in range(3)
                for b in range(3)
            ],
            axis=0,
        )
        gfull[d] = fold_cells(mm(kt[...], stack), FINE_W).astype(BF)
        return carry

    lax.fori_loop(0, 8, finish, 0)
    act[...] = full[1:7]
    gsk[...] = gfull[1:7]
    ds1[...] = pre[3:9]
    fx[...] = planes[2:8, 0:32, 128:896]
    cot[...] = planes[3:7, 32:64, 256:768]
    r = iota((512, 128), 0)
    goal = (r // 256) * 64 + lax.rem(r, 128) // 2
    pooling = (goal == iota((512, 128), 1)).astype(F32).astype(BF)
    for m in range(4):
        one = mm(full[2 * m, :, 128:640], pooling) + mm(full[2 * m + 1, :, 128:640], pooling)
        mid[m, 0:32, :] = (one * 0.125).astype(BF)
        two = mm(gfull[2 * m, :, 128:640], pooling) + mm(gfull[2 * m + 1, :, 128:640], pooling)
        mid[m, 32:64, :] = two.astype(BF)


def down_kernel(g, kdown, bias, out, ds2):
    lanes = 128 * g.shape[0]
    wide = [widened(gathered(g, m, 0, 32), MID_W) for m in range(4)]
    pooled = None
    pooling = pool_matrix(lanes, MID_W)
    for p in range(2):
        pre = None
        for a in range(3):
            y = mm(kdown[192 * a : 192 * a + 192, :], wide[p + a])
            part = shifted(y[0:64], -1, 0, MID_W) + y[64:128] + shifted(y[128:192], 1, 0, MID_W)
            pre = part if pre is None else pre + part
        pre = pre + bias[...]
        s = gate(pre)
        acted = (pre * s).astype(BF)
        out[:, p * lanes : (p + 1) * lanes] = acted
        ds2[:, p * lanes : (p + 1) * lanes] = (s * (1.0 + pre * (1.0 - s))).astype(BF)
        part = mm(acted, pooling)
        pooled = part if pooled is None else pooled + part
    out[:, 2 * lanes :] = (pooled * 0.125).astype(BF)


def core_kernel(nd, idx, own, lf, rt, p2l, p2r, g, kcoarse, kup, proj, b_coarse, b_up, act4, gp4, merged, snd, gs, kt):
    dep = idx[0]
    lanes = 128 * g.shape[0]
    small = lanes // 4
    pools = [p2l[...], lf[:, 2 * lanes :], own[:, 2 * lanes :], rt[:, 2 * lanes :], p2r[...]]
    wide = [widened(v, COARSE_W) for v in pools]
    spreading = spread_matrix(lanes, MID_W)
    ds3 = None
    lifts = []
    for q in range(3):
        pre = None
        for a in range(3):
            y = mm(kcoarse[192 * a : 192 * a + 192, :], wide[q + a])
            part = shifted(y[0:64], -1, 0, COARSE_W) + y[64:128] + shifted(y[128:192], 1, 0, COARSE_W)
            pre = part if pre is None else pre + part
        pre = pre + b_coarse[...]
        s = gate(pre)
        at = dep + q - 1
        acted = jnp.where((at >= 0) & (at < nd), pre * s, 0.0).astype(BF)
        lifts.append(mm(acted, spreading))
        if q == 1:
            ds3 = s * (1.0 + pre * (1.0 - s))
    wide = []
    for k in range(6):
        src = (lf, own, rt)[k // 2]
        start = (k % 2) * lanes
        plane = (src[:, start : start + lanes].astype(F32) + lifts[k // 2]).astype(BF)
        if 1 <= k < 5:
            merged[k - 1] = plane
        wide.append(widened(plane, MID_W))
    kt[...] = turned(kup[...])
    for p in range(4):
        pre = None
        for a in range(3):
            y = mm(kup[192 * a : 192 * a + 192, :], wide[p + a])
            part = shifted(y[0:64], -1, 0, MID_W) + y[64:128] + shifted(y[128:192], 1, 0, MID_W)
            pre = part if pre is None else pre + part
        pre = pre + b_up[...]
        s = gate(pre)
        act4[p] = (pre * s).astype(BF)
        at = 2 * dep + p - 1
        slope = jnp.where((at >= 0) & (at < 2 * nd), s * (1.0 + pre * (1.0 - s)), 0.0)
        grad = (mm(proj[...], gathered(g, p, 32, 64)) * slope).astype(BF)
        if 1 <= p < 3:
            gp4[p - 1] = grad
        gs[p] = row_taps(grad, MID_W)
    pooling = pool_matrix(lanes, MID_W)
    pooled = None
    for q in range(2):
        stack = jnp.concatenate([gs[q + 2 - a] for a in range(3)], axis=0)
        gm = fold_cells(mm(kt[...], stack), MID_W)
        high, low = split(gm)
        snd[:, q * lanes : (q + 1) * lanes] = high
        part = mm(high, pooling) + mm(low, pooling)
        pooled = part if pooled is None else pooled + part
    snd[:, 2 * lanes :] = (pooled * ds3).astype(BF)


def decode_kernel(
    nd, nh, idx, act4, gp4, merged, snd, own, lf, rt, g, act, cot, kout, proj, b_out,
    dec, d_up, d_coarse, d_out, d_proj, d_bias, pad, skip, gpad, acc,
):
    dep, hei = idx[0], idx[1]
    lanes = 128 * g.shape[0]
    small = lanes // 4
    own_at = pl.ds(pl.multiple_of(128 * hei, 128), 128)
    spreading = window_spread()
    h_at = iota((1, 768), 1) // FINE_W - 1 + 4 * hei
    h_in = (h_at >= 0) & (h_at < 4 * nh)
    for p in range(4):
        fill_padded(pad, p, act4[p])
        raised = mm(window(pad, p, hei), spreading).astype(BF)
        lifted = lax.dot_general(proj[...], raised, (((0,), (0,)), ((), ())), preferred_element_type=F32)
        for e in (2 * p - 1, 2 * p):
            if 0 <= e < 6:
                at = 4 * dep + e - 1
                inside = h_in & (at >= 0) & (at < 4 * nd)
                skip[e] = jnp.where(inside, act[e].astype(F32) + lifted, 0.0).astype(BF)
    for k in range(8):
        if 2 <= k < 6:
            plane = cot[k - 2]
            blank = jnp.zeros((32, 128), BF)
            for b in range(3):
                gpad[k, 32 * b : 32 * b + 32, :] = jnp.concatenate(
                    [blank] * b + [plane] + [blank] * (2 - b), axis=1
                )
        else:
            gpad[k] = jnp.zeros((96, 768), BF)
    acc[...] = jnp.zeros_like(acc)
    d_out[...] = jnp.zeros_like(d_out)

    def plane_step(e, carry):
        wide = widened(skip[e], FINE_W)
        y = mm(kout[...], wide)
        for a in range(3):
            part = y[96 * a : 96 * a + 32, 0:512]
            for b in (1, 2):
                part += y[96 * a + 32 * b : 96 * a + 32 * b + 32, 128 * b : 128 * b + 512]
            acc[e - a + 2] += part
        stack = jnp.concatenate([gpad[e + 2], gpad[e + 1], gpad[e]], axis=0)
        d_out[...] += mm_nt(stack, wide)
        return carry

    lax.fori_loop(0, 6, plane_step, 0)
    for d in range(4):
        dec[d] = (acc[d + 2] + b_out[...]).astype(BF)
    grads = jnp.concatenate([gp4[0, :, own_at], gp4[1, :, own_at]], axis=1)
    taps = []
    for p in range(4):
        fill_padded(pad, p, merged[p])
        taps.append(tap_windows(window(pad, p, hei)))
    for a in range(3):
        for b in range(3):
            d_up[3 * a + b] = mm_nt(grads, jnp.concatenate([taps[a][b], taps[a + 1][b]], axis=1))
    acts = jnp.concatenate([act4[1, :, own_at], act4[2, :, own_at]], axis=1)
    lifts = jnp.concatenate([g[hei, 1, 32:64, :], g[hei, 2, 32:64, :]], axis=1)
    d_proj[...] = mm_nt(acts, lifts)
    mine = iota((1, small), 1) // COARSE_W == hei
    third = jnp.where(mine, snd[:, 2 * lanes :].astype(F32), 0.0)
    third_b = third.astype(BF)
    for a, src in enumerate((lf, own, rt)):
        plane = src[:, 2 * lanes :].astype(F32)
        for b in range(3):
            cols = jnp.concatenate(
                [shifted(plane, b - 1, c - 1, COARSE_W).astype(BF) for c in range(3)], axis=0
            )
            d_coarse[3 * a + b] = mm_nt(third_b, cols)
    d_bias[0:64, :] = jnp.broadcast_to(jnp.sum(third, axis=1, keepdims=True), (64, 128))
    d_bias[64:128, :] = jnp.broadcast_to(jnp.sum(grads.astype(F32), axis=1, keepdims=True), (64, 128))
    total = sum(jnp.sum(cot[d].astype(F32), axis=1, keepdims=True) for d in range(4))
    d_bias[128:160, :] = jnp.broadcast_to(total, (32, 128))


def back_kernel(
    idx, own, lf, rt, g3l, g3r, ds_own, ds_lf, ds_rt, g, gsk, ds1, fx, kcoarse, kdown,
    gp1, d_in, d_down, d_bias, pad, pad1, gs2, gpad, kct, kdt,
):
    hei = idx[1]
    lanes = 128 * g.shape[0]
    thirds = [g3l[...], lf[:, 2 * lanes :], own[:, 2 * lanes :], rt[:, 2 * lanes :], g3r[...]]
    taps = [row_taps(v, COARSE_W) for v in thirds]
    kct[...] = turned(kcoarse[...])
    kdt[...] = turned(kdown[...])
    spreading = spread_matrix(lanes, MID_W)
    grads = []
    for q in range(3):
        stack = jnp.concatenate([taps[q + 2 - a] for a in range(3)], axis=0)
        high, low = split(fold_cells(mm(kct[...], stack), COARSE_W))
        lifted = (mm(high, spreading) + mm(low, spreading)) * 0.125
        src, slope = ((lf, ds_lf), (own, ds_own), (rt, ds_rt))[q]
        for k in range(2):
            at = slice(k * lanes, (k + 1) * lanes)
            plane = ((src[:, at].astype(F32) + lifted) * slope[:, at].astype(F32)).astype(BF)
            fill_padded(pad, 0, plane)
            win = window(pad, 0, hei)
            gs2[2 * q + k] = row_taps(win, MID_W)
            if q == 1:
                grads.append(win[:, 128:256])
    raising = window_spread()
    for p in range(4):
        stack = jnp.concatenate([gs2[p + 2 - a] for a in range(3)], axis=0)
        high, low = split(fold_cells(mm(kdt[...], stack), MID_W))
        raised = (mm(high, raising) + mm(low, raising)) * 0.125
        for e in (2 * p - 1, 2 * p):
            if 0 <= e < 6:
                gp1[e] = ((gsk[e].astype(F32) + raised) * ds1[e]).astype(BF)
    taps = []
    for p in range(4):
        fill_padded(pad1, 0, gathered(g, p, 0, 32))
        taps.append(tap_windows(window(pad1, 0, hei)))
    both = jnp.concatenate(grads, axis=1)
    for a in range(3):
        for b in range(3):
            d_down[3 * a + b] = mm_nt(both, jnp.concatenate([taps[a][b], taps[a + 1][b]], axis=1))
    d_bias[32:96, :] = jnp.broadcast_to(jnp.sum(both.astype(F32), axis=1, keepdims=True), (64, 128))
    total = jnp.zeros((32, 1), F32)
    for k in range(8):
        if 2 <= k < 6:
            plane = gp1[k - 1, :, 128:640]
            total += jnp.sum(plane.astype(F32), axis=1, keepdims=True)
            blank = jnp.zeros((32, 128), BF)
            for b in range(3):
                gpad[k, 32 * b : 32 * b + 32, :] = jnp.concatenate(
                    [blank] * b + [plane] + [blank] * (2 - b), axis=1
                )
        else:
            gpad[k] = jnp.zeros((96, 768), BF)
    d_bias[0:32, :] = jnp.broadcast_to(total, (32, 128))
    d_in[...] = jnp.zeros_like(d_in)

    def plane_step(e, carry):
        stack = jnp.concatenate([gpad[e + 2], gpad[e + 1], gpad[e]], axis=0)
        d_in[...] += mm_nt(stack, widened(fx[e], FINE_W))
        return carry

    lax.fori_loop(0, 6, plane_step, 0)


def last_kernel(gp1, kin, out, kt):
    kt[...] = turned(kin[...])
    for d in range(4):
        stack = jnp.concatenate(
            [
                gp1[d + 2 - a, :, 128 * (2 - b) : 128 * (2 - b) + 512]
                for a in range(3)
                for b in range(3)
            ],
            axis=0,
        )
        out[d] = fold_cells(mm(kt[...], stack), FINE_W).astype(BF)


def run(body, outs, scratch, args, smem=0, flops=0, name=None):
    specs = [pl.BlockSpec(memory_space=pltpu.SMEM)] * smem
    specs += [pl.BlockSpec(memory_space=pltpu.VMEM)] * (len(args) - smem)
    moved = sum(a.size * a.dtype.itemsize for a in args) + sum(
        math.prod(s) * jnp.dtype(t).itemsize for s, t in outs
    )
    return pl.pallas_call(
        body,
        out_shape=[jax.ShapeDtypeStruct(s, t) for s, t in outs],
        in_specs=specs,
        out_specs=[pl.BlockSpec(memory_space=pltpu.VMEM)] * len(outs),
        scratch_shapes=[pltpu.VMEM(s, t) for s, t in scratch],
        compiler_params=pltpu.CompilerParams(vmem_limit_bytes=48 * 1024 * 1024),
        cost_estimate=pl.CostEstimate(flops=flops, bytes_accessed=moved, transcendentals=0),
        name=name,
    )(*args)


def reduced(items):
    sizes = [item.size for item in items]
    flat = jnp.concatenate([item.reshape(-1) for item in items]).astype(BF)
    across = lax.axis_size("height")
    along = lax.axis_size("depth")
    rows = -(-flat.size // (across * 128 * 16)) * 16
    flat = jnp.pad(flat, (0, across * rows * 128 - flat.size))
    parts = lax.all_to_all(flat.reshape(across, rows, 128), "height", 0, 0)
    share = jnp.sum(parts.astype(F32), axis=0).astype(BF)
    fine_rows = -(-rows // (along * 8)) * 8
    share = jnp.pad(share, ((0, along * fine_rows - rows), (0, 0)))
    parts = lax.all_to_all(share.reshape(along, fine_rows, 128), "depth", 0, 0)
    own = jnp.sum(parts.astype(F32), axis=0).astype(BF)
    share = lax.all_to_all(jnp.broadcast_to(own, (along, fine_rows, 128)), "depth", 0, 0)
    share = share.reshape(along * fine_rows, 128)[:rows]
    total = lax.all_to_all(jnp.broadcast_to(share, (across, rows, 128)), "height", 0, 0)
    total = total.reshape(-1)
    out = []
    at = 0
    for item, size in zip(items, sizes):
        out.append(total[at : at + size].reshape(item.shape).astype(F32))
        at += size
    return out


def both_ways(axis, to_next, to_last, step=1):
    count = lax.axis_size(axis)
    up = [(i, i + step) for i in range(count - step)]
    down = [(i + step, i) for i in range(count - step)]
    return lax.ppermute(to_next, axis, up), lax.ppermute(to_last, axis, down)


def local(
    features,
    kernel_in,
    kernel_down,
    kernel_coarse,
    kernel_up,
    kernel_out,
    projection,
    biases,
    cotangent,
):
    nd = lax.axis_size("depth")
    nh = lax.axis_size("height")
    lanes = 128 * nh
    small = lanes // 4
    kin = kernel_in.reshape(288, 96)
    kout = kernel_out.reshape(288, 96)
    kdown = kernel_down.reshape(576, 96)
    kcoarse = kernel_coarse.reshape(576, 192)
    kup = kernel_up.reshape(576, 192)
    column = biases[:, None]
    scale = 1.0 / math.sqrt(features.shape[1] * features.shape[2] * features.shape[3] * nd * nh)
    idx = jnp.stack([lax.axis_index("depth"), lax.axis_index("height")]).astype(jnp.int32)

    x = jnp.concatenate([features, cotangent], axis=0).transpose(1, 2, 0, 3)
    low, high = both_ways("height", x[:, 2:4], x[:, 0:2])
    x = jnp.concatenate([low, x, high], axis=1)
    low, high = both_ways("depth", x[1:4], x[0:3])
    act, ds1, gsk, fx, cot, mid = run(
        functools.partial(fine_kernel, nd, nh),
        [
            ((6, 32, 768), BF),
            ((6, 32, 768), F32),
            ((6, 32, 768), BF),
            ((6, 32, 768), BF),
            ((4, 32, 512), BF),
            ((4, 64, 128), BF),
        ],
        [
            ((10, 64, 1024), BF),
            ((12, 32, 768), F32),
            ((8, 32, 768), BF),
            ((8, 32, 768), BF),
            ((96, 288), BF),
        ],
        (idx, low, x, high, kin, kout, column[0:32]),
        smem=1,
        flops=10**9,
        name="fine",
    )
    g = lax.all_to_all(jnp.broadcast_to(mid[None], (nh, 4, 64, 128)), "height", 0, 0)
    own, ds2 = run(
        down_kernel,
        [((64, 2 * lanes + small), BF), ((64, 2 * lanes), BF)],
        [],
        (g, kdown, column[32:96]),
        flops=5 * 10**8,
        name="down",
    )
    lf, rt = both_ways("depth", own, own)
    p2l, p2r = both_ways("depth", own[:, 2 * lanes :], own[:, 2 * lanes :], 2)
    act4, gp4, merged, snd = run(
        functools.partial(core_kernel, nd),
        [
            ((4, 64, lanes), BF),
            ((2, 64, lanes), BF),
            ((4, 64, lanes), BF),
            ((64, 2 * lanes + small), BF),
        ],
        [((4, 192, lanes), BF), ((192, 576), BF)],
        (idx, own, lf, rt, p2l, p2r, g, kcoarse, kup, projection, column[96:160], column[160:224]),
        smem=1,
        flops=3 * 10**9,
        name="core",
    )
    slf, srt = both_ways("depth", snd, snd)
    s2l, s2r = both_ways("depth", snd[:, 2 * lanes :], snd[:, 2 * lanes :], 2)
    dlf, drt = both_ways("depth", ds2, ds2)
    dec, d_up, d_coarse, d_out, d_proj, bias_a = run(
        functools.partial(decode_kernel, nd, nh),
        [
            ((4, 32, 512), BF),
            ((9, 64, 192), F32),
            ((9, 64, 192), F32),
            ((288, 96), F32),
            ((64, 32), F32),
            ((160, 128), F32),
        ],
        [
            ((4, 64, lanes + 256), BF),
            ((6, 32, 768), BF),
            ((8, 96, 768), BF),
            ((8, 32, 512), F32),
        ],
        (idx, act4, gp4, merged, snd, own, lf, rt, g, act, cot, kout, projection, column[224:256]),
        smem=1,
        flops=10**9,
        name="decode",
    )
    gp1, d_in, d_down, bias_b = run(
        back_kernel,
        [((6, 32, 768), BF), ((288, 96), F32), ((9, 64, 96), F32), ((96, 128), F32)],
        [
            ((1, 64, lanes + 256), BF),
            ((1, 32, lanes + 256), BF),
            ((6, 192, 384), BF),
            ((8, 96, 768), BF),
            ((192, 576), BF),
            ((96, 576), BF),
        ],
        (idx, snd, slf, srt, s2l, s2r, ds2, dlf, drt, g, gsk, ds1, fx, kcoarse, kdown),
        smem=1,
        flops=10**9,
        name="back",
    )
    (gfeat,) = run(
        last_kernel,
        [((4, 32, 512), BF)],
        [((96, 288), BF)],
        (gp1, kin),
        flops=10**8,
        name="last",
    )
    sums = jnp.concatenate([bias_b[:, 0], bias_a[:, 0]])
    summed = reduced((d_in, d_down, d_coarse, d_up, d_out, d_proj, sums))
    grads = [item * scale for item in summed]

    def placed(v):
        return v.reshape(4, 32, 4, 128).transpose(1, 0, 2, 3)

    return (
        placed(dec),
        placed(gfeat),
        *[item.reshape(-1) for item in grads[:5]],
        grads[5],
        grads[6],
    )


def solution(mesh):
    placed = (
        P(None, "depth", "height", None),
        P(),
        P(),
        P(),
        P(),
        P(),
        P(),
        P(),
        P(None, "depth", "height", None),
    )
    return jax.shard_map(
        local,
        mesh=mesh,
        in_specs=placed,
        out_specs=(
            P(None, "depth", "height", None),
            P(None, "depth", "height", None),
            P(),
            P(),
            P(),
            P(),
            P(),
            P(),
            P(),
        ),
        check_vma=False,
    )
```

time: 356 us -> 231 us (0.65)
  starting transfers between devices: 184 us -> 53.9 us
  blocking collectives: 0 us -> 73.9 us
  waiting for transfers between devices: 66.2 us -> 25.6 us
  matrix products: 35.6 us -> 0 us
  Pallas kernels: 0 us -> 29.5 us
  other arithmetic: 18.5 us -> 4.89 us
  local copies, waits for them, and re-layouts: 47 us -> 40.2 us
    all_to_all x0 -> x3, blocking collectives: none -> 73.9 us  [the longest x1 42.8 us: reduced(): parts = lax.all_to_all(share.reshape(along, fine_rows, 128), 'depth', 0, 0)]
    ppermute x40 -> x14, starting transfers between devices: 116 us -> 43.7 us  [both_ways(): return (lax.ppermute(to_next, axis, up), lax.ppermute(to_last, axis, down))]
    all_to_all x3 -> x1, starting transfers between devices: 62.3 us -> 6.65 us  [local(): lax.all_to_all(jnp.broadcast_to(mid[None], (nh, 4, 64, 128)), 'height', 0...]
    dot_general x138 -> x0, matrix products: 35.6 us -> none  [the longest x90 20.3 us: conv_taps(): jnp.einsum('ok,kdhw->odhw', kern[tap_depth, tap_height], window, preferre...]
    pallas_call x0 -> x6, Pallas kernels: none -> 29.5 us  [run(): pl.pallas_call(body, out_shape=[jax.ShapeDtypeStruct(s, t) for s, t in ou...]
    ppermute x40 -> x14, waiting for transfers between devices: 32.6 us -> 9.6 us  [both_ways(): return (lax.ppermute(to_next, axis, up), lax.ppermute(to_last, axis, down))]
    all_to_all x3 -> x1, waiting for transfers between devices: 24.9 us -> 6.77 us  [local(): lax.all_to_all(jnp.broadcast_to(mid[None], (nh, 4, 64, 128)), 'height', 0...]
    unnamed x77 -> x68, local copies, waits for them, and re-layouts: 3.99 us -> 18.2 us
  transfers between devices with their start and end apart: 44 -> 16, of which waited for: 15 -> 6; matrix products, arithmetic and copies ran while one was open for 16% -> 5% of each run, Pallas kernels for 0% -> 5%
where the time goes in v2:
time: 231 us; the launch traced here: 229 us
  blocking collectives  73.9 us (32%)
  starting transfers between devices  53.9 us (23%)
  local copies, waits for them, and re-layouts  40.2 us (17%)
  Pallas kernels  29.5 us (13%)
  waiting for transfers between devices  25.6 us (11%)
  other arithmetic  4.89 us (2%)
    ppermute x14, starting transfers between devices, both_ways(): return (lax.ppermute(to_next, axis, up), lax.ppermute(to_last, axis, down))  43.7 us
    all_to_all x1, blocking collectives, reduced(): parts = lax.all_to_all(share.reshape(along, fine_rows, 128), 'depth', 0, 0)  42.8 us
    pallas_call x6, Pallas kernels, run(): pl.pallas_call(body, out_shape=[jax.ShapeDtypeStruct(s, t) for s, t in ou...  29.5 us
    unnamed x68, local copies, waits for them, and re-layouts  18.2 us
    all_to_all x1, blocking collectives, reduced(): lax.all_to_all(jnp.broadcast_to(own, (along, fine_rows, 128)), 'depth', 0...  16.9 us
    all_to_all x1, blocking collectives, reduced(): parts = lax.all_to_all(flat.reshape(across, rows, 128), 'height', 0, 0)  14.2 us
    ppermute x14, waiting for transfers between devices, both_ways(): return (lax.ppermute(to_next, axis, up), lax.ppermute(to_last, axis, down))  9.6 us
    all_to_all x1, waiting for transfers between devices, reduced(): lax.all_to_all(jnp.broadcast_to(share, (across, rows, 128)), 'height', 0, 0)  9.2 us
  transfers between devices with their start and end apart: 16, of which 6 were waited for; matrix products, arithmetic and copies ran while one was open for 5% of the time, Pallas kernels for 5%

profile of v2, /device:TPU:1, one launch (start us, length us, event | category | flops | bytes accessed | tf_op | source)
XLA Modules:
  0.0 229.2 jit_solution(5587549726374179082)
XLA Ops:
  2.7 4.0 %collective-permute-start = (bf16[4,2,64,128]{3,2,1,0:T(8,128)(2,1)S(1)}, bf16[4,2,64,128]{3,2,1,0:T(8,128)(2,1)S(1)}, u32[]{:S(2)}, u32[]{:S(2)}) collective-permute-start(bf16[4,2,64,128]{3,2,1,0:T(8,128)(2,1)S(1)} %get-tuple-element.77), channel_id=1, source_target_pairs={{0,1},{1,2},{2,3},{3,4},{4,5},{5,6},{6,7},{8,9},{9,10},{10,11},{11... | collective-permute-start | bytes 393224 | tf_op jit(solution)/shard_map/ppermute | solution.py:470
  8.5 3.8 %collective-permute-done.1 = bf16[4,2,64,128]{3,2,1,0:T(8,128)(2,1)S(1)} collective-permute-done((bf16[4,2,64,128]{3,2,1,0:T(8,128)(2,1)S(1)}, bf16[4,2,64,128]{3,2,1,0:T(8,128)(2,1)S(1)}, u32[]{:S(2)}, u32[]{:S(2)}) %collective-permute-start.1) | collective-permute-done | bytes 131104 | tf_op jit(solution)/shard_map/ppermute | solution.py:470
  12.5 5.2 %collective-permute-start.2 = (bf16[3,8,64,128]{3,2,1,0:T(8,128)(2,1)S(1)}, bf16[3,8,64,128]{3,2,1,0:T(8,128)(2,1)S(1)}, u32[]{:S(2)}, u32[]{:S(2)}) collective-permute-start(bf16[3,8,64,128]{3,2,1,0:T(8,128)(2,1)S(1)} %get-tuple-element.76), channel_id=1, source_target_pairs={{0,8},{8,16},{16,24},{24,32},{32,40},{40,48},{48,56},{56,64},{64,7... | collective-permute-start | bytes 1179656 | tf_op jit(solution)/shard_map/ppermute | solution.py:470
  17.7 3.4 %collective-permute-start.3 = (bf16[3,8,64,128]{3,2,1,0:T(8,128)(2,1)S(1)}, bf16[3,8,64,128]{3,2,1,0:T(8,128)(2,1)S(1)}, u32[]{:S(2)}, u32[]{:S(2)}) collective-permute-start(bf16[3,8,64,128]{3,2,1,0:T(8,128)(2,1)S(1)} %get-tuple-element.75), channel_id=1, source_target_pairs={{8,0},{16,8},{24,16},{32,24},{40,32},{48,40},{56,48},{64,56},{72,6... | collective-permute-start | bytes 1179656 | tf_op jit(solution)/shard_map/ppermute | solution.py:470
  22.4 4.4 %collective-permute-done.3.xr = bf16[3,8,64,128]{3,2,1,0:T(8,128)(2,1)S(1)} collective-permute-done((bf16[3,8,64,128]{3,2,1,0:T(8,128)(2,1)S(1)}, bf16[3,8,64,128]{3,2,1,0:T(8,128)(2,1)S(1)}, u32[]{:S(2)}, u32[]{:S(2)}) %collective-permute-start.3) | collective-permute-done | bytes 393248 | tf_op jit(solution)/shard_map/ppermute | solution.py:470
  26.8 7.7 %fine.1 = (bf16[6,32,768]{2,1,0:T(8,128)(2,1)S(1)}, f32[6,32,768]{2,1,0:T(8,128)S(1)}, bf16[6,32,768]{2,1,0:T(8,128)(2,1)S(1)}, bf16[6,32,768]{2,1,0:T(8,128)(2,...) custom-call(s32[2]{0:T(128)S(1)} %pad_add_fusion.idx, ...), custom_call_target="tpu_custom_call" | custom-call | flops 1000000000 | bytes 3092616 | tf_op jit(solution)/shard_map/fine/pallas_call | solution.py:429
  35.5 6.7 %all-to-all-start = ((bf16[8,4,64,128]{3,2,1,0:T(8,128)(2,1)}), bf16[8,4,64,128]{3,2,1,0:T(8,128)(2,1)S(1)}, u32[]{:S(2)}, u32[]{:S(2)}) async-start(bf16[8,4,64,128]{3,2,1,0:T(8,128)(2,1)} %broadcast_in_dim.6), calls=%async_computation | async-start | bytes 1048576 | tf_op jit(solution)/shard_map/all_to_all | solution.py:523
  42.5 6.8 %all-to-all-done.g = bf16[8,4,64,128]{3,2,1,0:T(8,128)(2,1)S(1)} async-done(((bf16[8,4,64,128]{3,2,1,0:T(8,128)(2,1)}), bf16[8,4,64,128]{3,2,1,0:T(8,128)(2,1)S(1)}, u32[]{:S(2)}, u32[]{:S(2)}) %all-to-all-start) | async-done | bytes 524320 | tf_op jit(solution)/shard_map/all_to_all | solution.py:523
  49.3 2.1 down.1
  51.4 4.8 %collective-permute-start.4 = (bf16[64,2304]{1,0:T(8,128)(2,1)S(1)}, bf16[64,2304]{1,0:T(8,128)(2,1)S(1)}, u32[]{:S(2)}, u32[]{:S(2)}) collective-permute-start(bf16[64,2304]{1,0:T(8,128)(2,1)S(1)} %get-tuple-element.32.own), channel_id=1, source_target_pairs={{0,8},{8,16},{16,24},{24,32},{32,40},{40,48},{48,56},{56,64},{64,7... | collective-permute-start | bytes 884744 | tf_op jit(solution)/shard_map/ppermute | solution.py:470
  58.8 3.1 %collective-permute-start.6 = (bf16[64,256]{1,0:T(8,128)(2,1)}, bf16[64,256]{1,0:T(8,128)(2,1)S(1)}, u32[]{:S(2)}, u32[]{:S(2)}) collective-permute-start(bf16[64,256]{1,0:T(8,128)(2,1)} %slice.100), channel_id=1, source_target_pairs={{0,16},{8,24},{16,32},{24,40},{32,48},{40,56},{48,64},{56,72},{64,... | collective-permute-start | bytes 98312 | tf_op jit(solution)/shard_map/ppermute | solution.py:470
  64.9 5.0 %collective-permute-start.12 = (bf16[64,2048]{1,0:T(8,128)(2,1)}, bf16[64,2048]{1,0:T(8,128)(2,1)}, u32[]{:S(2)}, u32[]{:S(2)}) collective-permute-start(bf16[64,2048]{1,0:T(8,128)(2,1)} %get-tuple-element.40.ds_own), channel_id=1, source_target_pairs={{0,8},{8,16},{16,24},{24,32},{32,40},{40,48},{48,56},{56,64},{64,7... | collective-permute-start | bytes 786440 | tf_op jit(solution)/shard_map/ppermute | solution.py:470
  71.8 6.2 %core.1 = (bf16[4,64,1024]{2,1,0:T(8,128)(2,1)S(1)}, bf16[2,64,1024]{2,1,0:T(8,128)(2,1)S(1)}, bf16[4,64,1024]{2,1,0:T(8,128)(2,1)S(1)}, bf16[64,2304]{1,0:T(8,128)(2,1)S(1)}) custom-call(s32[2]{0:T(128)S(1)} %pad_add_fusion.idx, bf16[64,2304]{1,0:T(8,128)(2,1)S(1)} %get-tuple-element.32.own, bf16[64,2304]{1,0:T(8,128)(2,1)S(1)} %collective-permute-done.4.lf, ...), custom_call_target="tpu_custom_call" | custom-call | flops 3000000000 | bytes 3527176 | tf_op jit(solution)/shard_map/core/pallas_call | solution.py:429
  82.3 2.4 %collective-permute-start.9 = (bf16[64,2304]{1,0:T(8,128)(2,1)S(1)}, bf16[64,2304]{1,0:T(8,128)(2,1)}, u32[]{:S(2)}, u32[]{:S(2)}) collective-permute-start(bf16[64,2304]{1,0:T(8,128)(2,1)S(1)} %get-tuple-element.36.snd.own), channel_id=1, source_target_pairs={{8,0},{16,8},{24,16},{32,24},{40,32},{48,40},{56,48},{64,56},{72,6... | collective-permute-start | bytes 884744 | tf_op jit(solution)/shard_map/ppermute | solution.py:470
  88.0 6.1 %collective-permute-start.10 = (bf16[64,256]{1,0:T(8,128)(2,1)}, bf16[64,256]{1,0:T(8,128)(2,1)}, u32[]{:S(2)}, u32[]{:S(2)}) collective-permute-start(bf16[64,256]{1,0:T(8,128)(2,1)} %slice.107), channel_id=1, source_target_pairs={{0,16},{8,24},{16,32},{24,40},{32,48},{40,56},{48,64},{56,72},{64,... | collective-permute-start | bytes 98312 | tf_op jit(solution)/shard_map/ppermute | solution.py:470
  104.2 5.5 %decode.1 = (bf16[4,32,512]{2,1,0:T(8,128)(2,1)S(1)}, f32[9,64,192]{2,1,0:T(8,128)S(1)}, f32[9,64,192]{2,1,0:T(8,128)S(1)}, f32[288,96]{1,0:T(8,128)S(1)}, f32[64,32]{1,0:T(8,128)S(1)}, /*index=5*/f32[160,128]{1,0:T(8,128)S(1)}) custom-call(s32[2]{0:T(128)S(1)} %pad_add_fusion.idx, bf16[4,64,1024]{2,1,0:T(8,128)(2,1)S(1)} %copy-done.16, ...), custom_call_target="tpu_custom_call" | custom-call | flops 1000000000 | bytes 4716680 | tf_op jit(solution)/shard_map/decode/pallas_call | solution.py:429
  113.1 2.0 reshape.110
  119.5 7.2 %back.1 = (bf16[6,32,768]{2,1,0:T(8,128)(2,1)S(1)}, f32[288,96]{1,0:T(8,128)S(1)}, f32[9,64,96]{2,1,0:T(8,128)S(1)}, f32[96,128]{1,0:T(8,128)S(1)}) custom-call(s32[2]{0:T(128)S(1)} %pad_add_fusion.idx, bf16[64,2304]{1,0:T(8,128)(2,1)S(1)} %get-tuple-element.36.snd.own, bf16[64,2304]{1,0:T(8,128)(2,1)S(1)} %collective-permute-done.8.lf, ...), custom_call_target="tpu_custom_call" | custom-call | flops 1000000000 | bytes 4448264 | tf_op jit(solution)/shard_map/back/pallas_call | solution.py:429
  127.3 6.2 %concatenate.12 = bf16[334080]{0:T(1024)(128)(2,1)S(1)} concatenate(bf16[27648]{0:T(1024)(128)(2,1)S(1)} %reshape.108, bf16[55296]{0:T(1024)(128)(2,1)S(1)} %reshape.109, bf16[110592]{0:T(1024)(128)(2,1)S(1)} %copy-done.25, bf16[110592]{0:T(1024)(128)(2,1)} %reshape.111, bf16[27648]{0:T(1024)(128)(2,1)} %reshape.112, bf16[2048]{0:T(1024)(128)(2,1)S(1)} %reshape.113, ...), dimensions={0} | concatenate | bytes 1336320 | tf_op jit(solution)/shard_map/concatenate | solution.py:443
  133.6 14.2 %all_to_all.25 = bf16[8,336,128]{2,1,0:T(8,128)(2,1)S(1)} all-to-all(bf16[8,336,128]{2,1,0:T(8,128)(2,1)S(1)} %bitcast.27), channel_id=1, replica_groups=mesh['depth'=64,'height'=8] {'height'}, dimensions={0} | all-to-all | bytes 1376256 | tf_op jit(solution)/shard_map/all_to_all | solution.py:448
  148.0 42.8 %all_to_all.26 = bf16[64,8,128]{2,1,0:T(8,128)(2,1)S(1)} all-to-all(bf16[64,8,128]{2,1,0:T(8,128)(2,1)S(1)} %pad_bitcast_fusion), channel_id=1, replica_groups=mesh['depth'=64,'height'=8] {'depth'}, dimensions={0} | all-to-all | bytes 262144 | tf_op jit(solution)/shard_map/all_to_all | solution.py:452
  190.9 16.9 %all_to_all.27 = bf16[64,8,128]{2,1,0:T(8,128)(2,1)S(1)} all-to-all(bf16[64,8,128]{2,1,0:T(8,128)(2,1)S(1)} %broadcast_in_dim.14), channel_id=1, replica_groups=mesh['depth'=64,'height'=8] {'depth'}, dimensions={0} | all-to-all | bytes 262144 | tf_op jit(solution)/shard_map/all_to_all | solution.py:454
  208.7 3.5 %all-to-all-start.4 = ((bf16[8,336,128]{2,1,0:T(8,128)(2,1)}), bf16[8,336,128]{2,1,0:T(8,128)(2,1)S(1)}, u32[]{:S(2)}, u32[]{:S(2)}) async-start(bf16[8,336,128]{2,1,0:T(8,128)(2,1)} %broadcast_in_dim.15), calls=%async_computation.4 | async-start | bytes 1376256 | tf_op jit(solution)/shard_map/all_to_all | solution.py:456
  213.8 9.2 %all-to-all-done.4 = bf16[8,336,128]{2,1,0:T(8,128)(2,1)S(1)} async-done(((bf16[8,336,128]{2,1,0:T(8,128)(2,1)}), bf16[8,336,128]{2,1,0:T(8,128)(2,1)S(1)}, u32[]{:S(2)}, u32[]{:S(2)}) %all-to-all-start.4) | async-done | bytes 688160 | tf_op jit(solution)/shard_map/all_to_all | solution.py:456
  (139 shorter events, 48.5 us)
Async XLA Ops:
  0.7 20.6 %copy-start.29 = (bf16[27648]{0:T(1024)(128)(2,1)S(1)}, bf16[27648]{0:T(1024)(128)(2,1)}, u32[]{:S(2)}) copy-start(bf16[27648]{0:T(1024)(128)(2,1)} %param.14) | copy-start | bytes 165892
  0.7 20.7 %copy-start.31 = (f32[256]{0:T(256)S(1)}, f32[256]{0:T(256)}, u32[]{:S(2)}) copy-start(f32[256]{0:T(256)} %param.16) | copy-start | bytes 3076
  2.7 5.9 %collective-permute-start = (bf16[4,2,64,128]{3,2,1,0:T(8,128)(2,1)S(1)}, bf16[4,2,64,128]{3,2,1,0:T(8,128)(2,1)S(1)}, u32[]{:S(2)}, u32[]{:S(2)}) collective-permute-start(bf16[4,2,64,128]{3,2,1,0:T(8,128)(2,1)S(1)} %get-tuple-element.77), channel_id=1, source_target_pairs={{0,1},{1,2},{2,3},{3,4},{4,5},{5,6},{6,7},{8,9},{9,10},{10,11},{11... | collective-permute-start | bytes 393224 | tf_op jit(solution)/shard_map/ppermute | solution.py:470
  6.6 5.7 %collective-permute-start.1 = (bf16[4,2,64,128]{3,2,1,0:T(8,128)(2,1)S(1)}, bf16[4,2,64,128]{3,2,1,0:T(8,128)(2,1)S(1)}, u32[]{:S(2)}, u32[]{:S(2)}) collective-permute-start(bf16[4,2,64,128]{3,2,1,0:T(8,128)(2,1)S(1)} %get-tuple-element.78), channel_id=1, source_target_pairs={{1,0},{2,1},{3,2},{4,3},{5,4},{6,5},{7,6},{9,8},{10,9},{11,10},{12... | collective-permute-start | bytes 393224 | tf_op jit(solution)/shard_map/ppermute | solution.py:470
  12.5 9.9 %collective-permute-start.2 = (bf16[3,8,64,128]{3,2,1,0:T(8,128)(2,1)S(1)}, bf16[3,8,64,128]{3,2,1,0:T(8,128)(2,1)S(1)}, u32[]{:S(2)}, u32[]{:S(2)}) collective-permute-start(bf16[3,8,64,128]{3,2,1,0:T(8,128)(2,1)S(1)} %get-tuple-element.76), channel_id=1, source_target_pairs={{0,8},{8,16},{16,24},{24,32},{32,40},{40,48},{48,56},{56,64},{64,7... | collective-permute-start | bytes 1179656 | tf_op jit(solution)/shard_map/ppermute | solution.py:470
  17.7 9.1 %collective-permute-start.3 = (bf16[3,8,64,128]{3,2,1,0:T(8,128)(2,1)S(1)}, bf16[3,8,64,128]{3,2,1,0:T(8,128)(2,1)S(1)}, u32[]{:S(2)}, u32[]{:S(2)}) collective-permute-start(bf16[3,8,64,128]{3,2,1,0:T(8,128)(2,1)S(1)} %get-tuple-element.75), channel_id=1, source_target_pairs={{8,0},{16,8},{24,16},{32,24},{40,32},{48,40},{56,48},{64,56},{72,6... | collective-permute-start | bytes 1179656 | tf_op jit(solution)/shard_map/ppermute | solution.py:470
  21.2 21.1 %copy-start.27 = (bf16[55296]{0:T(1024)(128)(2,1)S(1)}, bf16[55296]{0:T(1024)(128)(2,1)}, u32[]{:S(2)}) copy-start(bf16[55296]{0:T(1024)(128)(2,1)} %param.11) | copy-start | bytes 331780
  21.4 21.1 %copy-start.2 = (bf16[288,96]{1,0:T(8,128)(2,1)}, bf16[288,96]{1,0:T(8,128)(2,1)S(1)}, u32[]{:S(2)}) copy-start(bf16[288,96]{1,0:T(8,128)(2,1)S(1)} %reshape.102.kout) | copy-start | bytes 165892
  34.6 28.9 %copy-start.26 = (bf16[110592]{0:T(1024)(128)(2,1)S(1)}, bf16[110592]{0:T(1024)(128)(2,1)}, u32[]{:S(2)}) copy-start(bf16[110592]{0:T(1024)(128)(2,1)} %param.12) | copy-start | bytes 663556
  34.6 29.1 %copy-start.30 = (bf16[64,32]{0,1:T(8,128)(2,1)S(1)}, bf16[64,32]{0,1:T(8,128)(2,1)}, u32[]{:S(2)}) copy-start(bf16[64,32]{0,1:T(8,128)(2,1)} %param.15) | copy-start | bytes 12292
  35.5 13.8 %all-to-all-start = ((bf16[8,4,64,128]{3,2,1,0:T(8,128)(2,1)}), bf16[8,4,64,128]{3,2,1,0:T(8,128)(2,1)S(1)}, u32[]{:S(2)}, u32[]{:S(2)}) async-start(bf16[8,4,64,128]{3,2,1,0:T(8,128)(2,1)} %broadcast_in_dim.6), calls=%async_computation | async-start | bytes 1048576 | tf_op jit(solution)/shard_map/all_to_all | solution.py:523
  51.4 26.6 %copy-start.8 = (bf16[64,2304]{1,0:T(8,128)(2,1)}, bf16[64,2304]{1,0:T(8,128)(2,1)S(1)}, u32[]{:S(2)}) copy-start(bf16[64,2304]{1,0:T(8,128)(2,1)S(1)} %get-tuple-element.32.own) | copy-start | bytes 884740
  51.4 18.6 %collective-permute-start.4 = (bf16[64,2304]{1,0:T(8,128)(2,1)S(1)}, bf16[64,2304]{1,0:T(8,128)(2,1)S(1)}, u32[]{:S(2)}, u32[]{:S(2)}) collective-permute-start(bf16[64,2304]{1,0:T(8,128)(2,1)S(1)} %get-tuple-element.32.own), channel_id=1, source_target_pairs={{0,8},{8,16},{16,24},{24,32},{32,40},{40,48},{48,56},{56,64},{64,7... | collective-permute-start | bytes 884744 | tf_op jit(solution)/shard_map/ppermute | solution.py:470
  56.3 13.8 %collective-permute-start.5 = (bf16[64,2304]{1,0:T(8,128)(2,1)S(1)}, bf16[64,2304]{1,0:T(8,128)(2,1)S(1)}, u32[]{:S(2)}, u32[]{:S(2)}) collective-permute-start(bf16[64,2304]{1,0:T(8,128)(2,1)S(1)} %get-tuple-element.32.own), channel_id=1, source_target_pairs={{8,0},{16,8},{24,16},{32,24},{40,32},{48,40},{56,48},{64,56},{72,6... | collective-permute-start | bytes 884744 | tf_op jit(solution)/shard_map/ppermute | solution.py:470
  58.8 11.2 %collective-permute-start.6 = (bf16[64,256]{1,0:T(8,128)(2,1)}, bf16[64,256]{1,0:T(8,128)(2,1)S(1)}, u32[]{:S(2)}, u32[]{:S(2)}) collective-permute-start(bf16[64,256]{1,0:T(8,128)(2,1)} %slice.100), channel_id=1, source_target_pairs={{0,16},{8,24},{16,32},{24,40},{32,48},{40,56},{48,64},{56,72},{64,... | collective-permute-start | bytes 98312 | tf_op jit(solution)/shard_map/ppermute | solution.py:470
  62.0 8.0 %collective-permute-start.7 = (bf16[64,256]{1,0:T(8,128)(2,1)}, bf16[64,256]{1,0:T(8,128)(2,1)S(1)}, u32[]{:S(2)}, u32[]{:S(2)}) collective-permute-start(bf16[64,256]{1,0:T(8,128)(2,1)} %slice.100), channel_id=1, source_target_pairs={{16,0},{24,8},{32,16},{40,24},{48,32},{56,40},{64,48},{72,56},{80,... | collective-permute-start | bytes 98312 | tf_op jit(solution)/shard_map/ppermute | solution.py:470
  64.9 46.0 %collective-permute-start.12 = (bf16[64,2048]{1,0:T(8,128)(2,1)}, bf16[64,2048]{1,0:T(8,128)(2,1)}, u32[]{:S(2)}, u32[]{:S(2)}) collective-permute-start(bf16[64,2048]{1,0:T(8,128)(2,1)} %get-tuple-element.40.ds_own), channel_id=1, source_target_pairs={{0,8},{8,16},{16,24},{24,32},{32,40},{40,48},{48,56},{56,64},{64,7... | collective-permute-start | bytes 786440 | tf_op jit(solution)/shard_map/ppermute | solution.py:470
  80.4 39.1 %collective-permute-start.8 = (bf16[64,2304]{1,0:T(8,128)(2,1)S(1)}, bf16[64,2304]{1,0:T(8,128)(2,1)S(1)}, u32[]{:S(2)}, u32[]{:S(2)}) collective-permute-start(bf16[64,2304]{1,0:T(8,128)(2,1)S(1)} %get-tuple-element.36.snd.own), channel_id=1, source_target_pairs={{0,8},{8,16},{16,24},{24,32},{32,40},{40,48},{48,56},{56,64},{64,7... | collective-permute-start | bytes 884744 | tf_op jit(solution)/shard_map/ppermute | solution.py:470
  82.3 37.2 %collective-permute-start.9 = (bf16[64,2304]{1,0:T(8,128)(2,1)S(1)}, bf16[64,2304]{1,0:T(8,128)(2,1)}, u32[]{:S(2)}, u32[]{:S(2)}) collective-permute-start(bf16[64,2304]{1,0:T(8,128)(2,1)S(1)} %get-tuple-element.36.snd.own), channel_id=1, source_target_pairs={{8,0},{16,8},{24,16},{32,24},{40,32},{48,40},{56,48},{64,56},{72,6... | collective-permute-start | bytes 884744 | tf_op jit(solution)/shard_map/ppermute | solution.py:470
  84.7 34.8 %collective-permute-start.13 = (bf16[64,2048]{1,0:T(8,128)(2,1)}, bf16[64,2048]{1,0:T(8,128)(2,1)}, u32[]{:S(2)}, u32[]{:S(2)}) collective-permute-start(bf16[64,2048]{1,0:T(8,128)(2,1)} %get-tuple-element.40.ds_own), channel_id=1, source_target_pairs={{8,0},{16,8},{24,16},{32,24},{40,32},{48,40},{56,48},{64,56},{72,6... | collective-permute-start | bytes 786440 | tf_op jit(solution)/shard_map/ppermute | solution.py:470
  88.0 31.5 %collective-permute-start.10 = (bf16[64,256]{1,0:T(8,128)(2,1)}, bf16[64,256]{1,0:T(8,128)(2,1)}, u32[]{:S(2)}, u32[]{:S(2)}) collective-permute-start(bf16[64,256]{1,0:T(8,128)(2,1)} %slice.107), channel_id=1, source_target_pairs={{0,16},{8,24},{16,32},{24,40},{32,48},{40,56},{48,64},{56,72},{64,... | collective-permute-start | bytes 98312 | tf_op jit(solution)/shard_map/ppermute | solution.py:470
  110.9 8.6 %collective-permute-start.11 = (bf16[64,256]{1,0:T(8,128)(2,1)}, bf16[64,256]{1,0:T(8,128)(2,1)}, u32[]{:S(2)}, u32[]{:S(2)}) collective-permute-start(bf16[64,256]{1,0:T(8,128)(2,1)} %slice.107), channel_id=1, source_target_pairs={{16,0},{24,8},{32,16},{40,24},{48,32},{56,40},{64,48},{72,56},{80,... | collective-permute-start | bytes 98312 | tf_op jit(solution)/shard_map/ppermute | solution.py:470
  133.6 78.6 %copy-start.1 = (bf16[4,32,512]{2,1,0:T(8,128)(2,1)S(1)}, bf16[4,32,512]{2,1,0:T(8,128)(2,1)}, u32[]{:S(2)}) copy-start(bf16[4,32,512]{2,1,0:T(8,128)(2,1)} %copy-done) | copy-start | bytes 393220
  208.7 14.3 %all-to-all-start.4 = ((bf16[8,336,128]{2,1,0:T(8,128)(2,1)}), bf16[8,336,128]{2,1,0:T(8,128)(2,1)S(1)}, u32[]{:S(2)}, u32[]{:S(2)}) async-start(bf16[8,336,128]{2,1,0:T(8,128)(2,1)} %broadcast_in_dim.15), calls=%async_computation.4 | async-start | bytes 1376256 | tf_op jit(solution)/shard_map/all_to_all | solution.py:456
  (24 other events, 83.6 us)
